TPU v7x, 32 devices: a whole 2x2x4 slice. The times are simulated.
32 devices in a mesh: req: 4 (over z), tp: 8 (over y, x, core).
Axes of the slice: x: 2, y: 2, z: 4, core: 2. Of those that a mesh axis runs over, the one named last changes fastest.
Arguments:
- queries: bfloat16 [1024, 32, 128], P('req', 'tp'), may hold values from -6 to 6
- key_new: bfloat16 [1024, 8, 128], P('req'), may hold values from -6 to 6
- value_new: bfloat16 [1024, 8, 128], P('req'), may hold values from -6 to 6
- cache_keys: bfloat16 [8, 1024, 8, 128], P('req', 'tp'), may hold values from -6 to 6
- cache_values: bfloat16 [8, 1024, 8, 128], P('req', 'tp'), may hold values from -6 to 6
- context_lengths: int32 [8], P('req'), may hold values from 1 to 1024, 4096 in all
- residual: bfloat16 [1024, 4096], P('req', 'tp'), may hold values from -8 to 8
- out_weight: bfloat16 [4096, 4096], P('tp'), may hold values from -0.125 to 0.125
- norm_gain: bfloat16 [4096], replicated, may hold values from 0.099609375 to 1.8984375
- router: bfloat16 [4096, 4], replicated, may hold values from -0.09375 to 0.09375
- routes: int32 [1024, 2], P('req'), may hold values from 0 to 3, all different within a row; in each aligned block of 256 rows (0 to 255, 256 to 511, ...) at most 256 rows name the same one
- gate_weight: bfloat16 [4, 4096, 14336], P('req', None, 'tp'), may hold values from -0.09375 to 0.09375
- up_weight: bfloat16 [4, 4096, 14336], P('req', None, 'tp'), may hold values from -0.09375 to 0.09375
- down_weight: bfloat16 [4, 14336, 4096], P('req', 'tp'), may hold values from -0.0625 to 0.0625
Outputs:
- layer_out: bfloat16 [1024, 4096], P('req', 'tp')
Inputs may be any that keep to these rules, and one draw needn't show every extreme that they name: `routes`: each row names two different experts. Among the rows of one index of req no expert is named by more than 256 rows, and in every draw some expert is named by exactly 256 rows of some index. `context_lengths`: some request uses all 1024 cached positions.
All inputs are finite; a program needn't handle non-finite values. No bound on the sum of `context_lengths` on one device may be relied on, other than what follows from the above.
Results may differ from a plain program's by a relative error of at most 0.015.
Values may be sent and summed in bfloat16 or wider, within the bound.
No kernel may reach another device: no remote copies, remote signals or barrier semaphores. Data moves between devices by JAX's collectives and lax.ppermute only.
A program may use at most 128 MiB of HBM per device.

v0:
```python
import jax
import jax.numpy as jnp
from jax import lax
from jax.sharding import PartitionSpec as P

norm_eps = 1e-05
masked_score = -1e30


def slot_places(route_block, experts, capacity):
    chosen = route_block.reshape(-1)
    indicator = (chosen[:, None] == jnp.arange(experts, dtype=jnp.int32)[None, :]).astype(jnp.int32)
    earlier = jnp.cumsum(indicator, axis=0) - indicator
    within = jnp.sum(earlier * indicator, axis=1)
    return chosen * capacity + within


def pick_logit(logits, column, experts):
    matches = column[:, None] == jnp.arange(experts, dtype=jnp.int32)[None, :]
    return jnp.sum(jnp.where(matches, logits, 0.0), axis=1)


def softmax_block(scores, allowed):
    scores = jnp.where(allowed, scores, masked_score)
    highest = jnp.max(scores, axis=-1)
    weights = jnp.where(allowed, jnp.exp(scores - highest[..., None]), 0.0)
    denominator = jnp.maximum(jnp.sum(weights, axis=-1), 1.0)
    return (weights.astype(jnp.bfloat16), denominator, highest + jnp.log(denominator))


def per_device(
    queries,
    key_new,
    value_new,
    cache_keys,
    cache_values,
    context_lengths,
    residual,
    out_weight,
    norm_gain,
    router,
    routes,
    gate_weight,
    up_weight,
    down_weight,
):
    head_devices = lax.axis_size("tp")
    expert_devices = lax.axis_size("req")
    head_rank = lax.axis_index("tp")
    local_rows = queries.shape[0]
    local_heads = queries.shape[1]
    head_width = queries.shape[2]
    local_requests = cache_keys.shape[0]
    local_context = cache_keys.shape[1]
    key_heads = cache_keys.shape[2]
    new_rows = local_rows // local_requests
    head_count = local_heads * head_devices
    grouping = head_count // key_heads
    scaling = head_width ** (-0.5)
    every_query = lax.all_gather(queries, "tp", axis=1, tiled=True)
    grouped = every_query.reshape(local_requests, new_rows, key_heads, grouping, head_width)
    far_scores = (
        jnp.einsum("rnkgd,rlkd->rnkgl", grouped, cache_keys, preferred_element_type=jnp.float32)
        * scaling
    )
    position = head_rank * local_context + jnp.arange(local_context, dtype=jnp.int32)
    far_allowed = (position[None, :] < context_lengths[:, None])[:, None, None, None, :]
    far_probs, far_denominator, far_logs = softmax_block(far_scores, far_allowed)
    far_mixture = (
        jnp.einsum("rnkgl,rlkd->rnkgd", far_probs, cache_values, preferred_element_type=jnp.float32)
        / far_denominator[..., None]
    )
    far_parts, part_logs = (
        lax.all_to_all(
            far_mixture.reshape(1, local_rows, head_count, head_width).astype(jnp.bfloat16),
            "tp",
            split_axis=2,
            concat_axis=0,
            tiled=True,
        ).astype(jnp.float32),
        lax.all_to_all(
            far_logs.reshape(1, local_rows, head_count).astype(jnp.bfloat16),
            "tp",
            split_axis=2,
            concat_axis=0,
            tiled=True,
        ).astype(jnp.float32),
    )
    own_heads = head_rank * local_heads + jnp.arange(local_heads, dtype=jnp.int32)
    selector = (
        (own_heads // grouping)[:, None] == jnp.arange(key_heads, dtype=jnp.int32)[None, :]
    ).astype(jnp.bfloat16)
    near_keys = (
        jnp.einsum("rkd,hk->rhd", key_new, selector, preferred_element_type=jnp.float32)
        .astype(jnp.bfloat16)
        .reshape(local_requests, new_rows, local_heads, head_width)
    )
    near_values = (
        jnp.einsum("rkd,hk->rhd", value_new, selector, preferred_element_type=jnp.float32)
        .astype(jnp.bfloat16)
        .reshape(local_requests, new_rows, local_heads, head_width)
    )
    own_query = queries.reshape(local_requests, new_rows, local_heads, head_width)
    near_scores = (
        jnp.einsum("rihd,rjhd->rhij", own_query, near_keys, preferred_element_type=jnp.float32)
        * scaling
    )
    new_steps = jnp.arange(new_rows, dtype=jnp.int32)
    near_allowed = (new_steps[None, :] <= new_steps[:, None])[None, None]
    near_probs, near_denominator, near_logs = softmax_block(near_scores, near_allowed)
    near_mixture = (
        jnp.einsum("rhij,rjhd->rihd", near_probs, near_values, preferred_element_type=jnp.float32)
        / jnp.transpose(near_denominator, (0, 2, 1))[..., None]
    )
    near_logs = jnp.transpose(near_logs, (0, 2, 1)).reshape(1, local_rows, local_heads)
    all_logs = jnp.concatenate([part_logs, near_logs], axis=0)
    all_mixture = jnp.concatenate(
        [far_parts, near_mixture.reshape(1, local_rows, local_heads, head_width)], axis=0
    )
    peak_log = jnp.max(all_logs, axis=0)
    blend_weights = jnp.exp(all_logs - peak_log[None])
    attention = (
        jnp.sum(blend_weights[..., None] * all_mixture, axis=0)
        / jnp.sum(blend_weights, axis=0)[..., None]
    ).astype(jnp.bfloat16)
    attention = attention.reshape(local_rows, local_heads * head_width)
    head_partial = jnp.dot(attention, out_weight, preferred_element_type=jnp.float32)
    model_width = out_weight.shape[1]
    slice_width = model_width // head_devices
    first_column = head_rank * slice_width
    attention_part = lax.psum_scatter(
        head_partial.astype(jnp.bfloat16), "tp", scatter_dimension=1, tiled=True
    ).astype(jnp.float32)
    hidden = (residual.astype(jnp.float32) + attention_part).astype(jnp.bfloat16)
    hidden_float = hidden.astype(jnp.float32)
    gain_part = lax.dynamic_slice_in_dim(norm_gain, first_column, slice_width, 0).astype(
        jnp.float32
    )
    router_part = lax.dynamic_slice_in_dim(router, first_column, slice_width, 0).astype(jnp.float32)
    scaled = hidden_float * gain_part[None, :]
    squares, raw_logits = lax.psum(
        (
            jnp.sum(hidden_float * hidden_float, axis=1),
            jnp.dot(scaled, router_part, precision=lax.Precision.HIGHEST),
        ),
        "tp",
    )
    inverse_rms = lax.rsqrt(squares[:, None] / model_width + norm_eps)
    normed_float = scaled * inverse_rms
    logits = raw_logits * inverse_rms
    logit_first = pick_logit(logits, routes[:, 0], expert_devices)
    logit_second = pick_logit(logits, routes[:, 1], expert_devices)
    weight_first = 1.0 / (1.0 + jnp.exp(logit_second - logit_first))
    weight_second = 1.0 / (1.0 + jnp.exp(logit_first - logit_second))
    normed = normed_float.astype(jnp.bfloat16)
    top_count = routes.shape[1]
    capacity = 4 * local_rows // expert_devices
    destination = slot_places(routes, expert_devices, capacity)
    pair_rows = jnp.repeat(jnp.arange(local_rows, dtype=jnp.int32), top_count)
    slot_source = (
        jnp.full((expert_devices * capacity,), local_rows, jnp.int32).at[destination].set(pair_rows)
    )
    padded = jnp.concatenate([normed, jnp.zeros((1, normed.shape[1]), jnp.bfloat16)], axis=0)
    outgoing = padded[slot_source].reshape(expert_devices, capacity, normed.shape[1])
    gate_matrix = gate_weight[0]
    up_matrix = up_weight[0]
    down_matrix = down_weight[0]
    incoming = lax.all_to_all(outgoing, "req", split_axis=0, concat_axis=0, tiled=True)
    fragment = lax.all_gather(incoming, "tp", axis=2, tiled=True)
    piece_width = fragment.shape[2]
    rows_in = fragment.reshape(-1, piece_width)
    gate_sums = jnp.dot(rows_in, gate_matrix, preferred_element_type=jnp.float32)
    up_sums = jnp.dot(rows_in, up_matrix, preferred_element_type=jnp.float32)
    activated = (jax.nn.silu(gate_sums) * up_sums).astype(jnp.bfloat16)
    expert_partial = jnp.dot(activated, down_matrix, preferred_element_type=jnp.float32)
    expert_result = lax.psum_scatter(
        expert_partial.astype(jnp.bfloat16), "tp", scatter_dimension=1, tiled=True
    )
    returned = lax.all_to_all(
        expert_result.reshape(expert_devices, capacity, slice_width),
        "req",
        split_axis=0,
        concat_axis=0,
        tiled=True,
    )
    result_pairs = (
        returned.reshape(expert_devices * capacity, slice_width)[destination]
        .reshape(local_rows, top_count, slice_width)
        .astype(jnp.float32)
    )
    combined = (
        hidden_float
        + weight_first[:, None] * result_pairs[:, 0]
        + weight_second[:, None] * result_pairs[:, 1]
    )
    return combined.astype(jnp.bfloat16)


def solution(mesh):
    placed = (
        P("req", "tp", None),
        P("req", None, None),
        P("req", None, None),
        P("req", "tp", None, None),
        P("req", "tp", None, None),
        P("req"),
        P("req", "tp"),
        P("tp", None),
        P(),
        P(),
        P("req", None),
        P("req", None, "tp"),
        P("req", None, "tp"),
        P("req", "tp", None),
    )
    return jax.shard_map(
        per_device, mesh=mesh, in_specs=placed, out_specs=P("req", "tp"), check_vma=False
    )
```

profile of v0, /device:TPU:8, one launch (start us, length us, event | category | flops | bytes accessed | tf_op | source)
XLA Modules:
  0.0 411.4 jit_solution(17872833492182340394)
XLA Ops:
  6.5 1.7 copy.61
  8.4 1.4 convolution_convert_fusion.2
  9.8 1.3 fusion.73
  11.2 0.7 broadcast_compare_fusion
  11.9 26.5 %all-gather.3.cloned.1.call-done = bf16[256,32,128]{2,0,1:T(8,128)(2,1)} async-done(((bf16[256,4,128]{2,0,1:T(8,128)(2,1)}), bf16[256,32,128]{2,0,1:T(8,128)(2,1)}) %all-gather.3.cloned.1.call-update) | async-done | bytes 2097168 | tf_op jit(solution)/shard_map/all_gather | solution.py:60
  38.3 2.6 bitcast_reduce_fusion
  41.0 1.9 copy-done.2
  42.9 1.4 fusion.16
  44.3 0.5 broadcast.192
  44.8 0.7 reduce.8
  45.5 0.6 reshape.304
  46.2 3.3 all-to-all-start
  49.5 4.2 %fusion.12 = bf16[2,128,8,4,128]{4,1,3,2,0:T(8,128)(2,1)S(1)} fusion(f32[2,8,128,128,4]{3,2,4,1,0:T(8,128)} %copy-done.2, f32[2,128,8,4]{1,3,2,0:T(4,128)S(1)} %get-tuple-element.16, f32[2,128,8,4]{1,3,2,0:T(4,128)S(1)} %get-tuple-element.23, pred[2,128]{1,0:T(4,128)(4,1)S(1)} %broadcast_compare_fusion, bf16[2,128,8,128,1]{3,2,1,0,4:T(8,128)(2,1)S(1)} %bitcast.139), kind=kOutput, calls=%fused_computation.16 | convolution fusion | flops 275775488 | bytes 6881536 | tf_op jit(solution)/shard_map/rnkgl,rlkd->rnkgd/dot_general | solution.py:70
  53.7 1.6 copy.70
  55.3 4.1 all-to-all-start.1
  59.5 0.4 convolution_convert_fusion.1
  59.9 0.3 fusion.26
  60.5 25.6 %all-to-all-done.1 = bf16[1,256,32,128]{3,1,0,2:T(8,128)(2,1)S(1)} async-done(((bf16[1,256,32,128]{3,1,0,2:T(8,128)(2,1)}), bf16[1,256,32,128]{3,1,0,2:T(8,128)(2,1)S(1)}, u32[]{:S(2)}, u32[]{:S(2)}) %all-to-all-start.1) | async-done | bytes 2097184 | tf_op jit(solution)/shard_map/all_to_all | solution.py:74
  86.1 0.5 convert_bitcast_fusion
  86.6 1.6 fusion.9
  88.2 0.2 divide_convert_fusion
  88.4 0.1 copy.76
  88.6 4.9 %convolution_convert_fusion = bf16[256,4096]{1,0:T(8,128)(2,1)} fusion(bf16[256,512]{0,1:T(8,128)(2,1)S(1)} %bitcast.146, bf16[512,4096]{1,0:T(8,128)(2,1)} %param.21), kind=kOutput, calls=%fused_computation.11 | convolution fusion | flops 1074790400 | bytes 6553600 | tf_op jit(solution)/shard_map/dot_general | solution.py:127
  93.7 0.1 eq.83
  94.0 1.2 reduce-window.6
  95.2 0.2 slice_reduce_fusion
  95.4 0.2 reduce-window.9
  95.7 0.1 mul.122
  96.2 2.4 scatter_custom_fusion
  98.6 0.8 dynamic-slice_convert_fusion
  99.4 34.6 %reduce-scatter.3.cloned.1.call-done = bf16[256,512]{1,0:T(8,128)(2,1)} async-done(((bf16[256,4096]{1,0:T(8,128)(2,1)}), bf16[256,512]{1,0:T(8,128)(2,1)}) %reduce-scatter.3.cloned.1.call-update) | async-done | bytes 262160 | tf_op jit(solution)/shard_map/reduce_scatter | solution.py:131
  134.0 1.1 fusion.32
  135.1 1.1 fusion.30
  136.1 13.0 %all-reduce.1 = (f32[256]{0:T(256)S(1)}, f32[256,4]{0,1:T(4,128)S(1)}) all-reduce(f32[256]{0:T(256)S(1)} %get-tuple-element.9, f32[256,4]{0,1:T(4,128)S(1)} %fusion.30), channel_id=1, replica_groups=mesh['req'=4,'tp'=8] {'tp'}, use_global_device_ids=true, to_apply=%region_10.11 | all-reduce | flops 1280 | bytes 10240 | tf_op jit(solution)/shard_map/psum | solution.py:141
  149.3 4.0 gather_fusion
  153.3 28.1 %all_to_all.34 = bf16[4,256,512]{2,1,0:T(8,128)(2,1)} all-to-all(bf16[4,256,512]{2,1,0:T(8,128)(2,1)S(1)} %bitcast.143), channel_id=1, replica_groups=mesh['req'=4,'tp'=8] {'req'}, dimensions={0} | all-to-all | bytes 2097152 | tf_op jit(solution)/shard_map/all_to_all | solution.py:168
  181.4 0.2 reduce-scatter.5.cloned.1.call-start
  181.6 55.2 %all-gather.5.cloned.1.call-done = bf16[4,256,4096]{2,1,0:T(8,128)(2,1)} async-done(((bf16[4,256,512]{2,1,0:T(8,128)(2,1)}), bf16[4,256,4096]{2,1,0:T(8,128)(2,1)}) %all-gather.5.cloned.1.call-update) | async-done | bytes 8388624 | tf_op jit(solution)/shard_map/all_gather | solution.py:169
  236.8 21.8 %fusion.4 = f32[1024,1792]{1,0:T(8,128)} fusion(bf16[1024,4096]{1,0:T(8,128)(2,1)} %bitcast.161, bf16[1,4096,1792]{2,1,0:T(8,128)(2,1)} %param.25), kind=kOutput, calls=%fused_computation.7 | convolution fusion | flops 15032385536 | bytes 30408704 | tf_op jit(solution)/shard_map/dot_general | solution.py:172
  258.6 23.5 %multiply_convert_fusion = bf16[1024,1792]{1,0:T(8,128)(2,1)} fusion(f32[1024,1792]{1,0:T(8,128)} %fusion.4, bf16[1024,4096]{1,0:T(8,128)(2,1)} %bitcast.162, bf16[1,4096,1792]{2,1,0:T(8,128)(2,1)} %param.26), kind=kOutput, calls=%fused_computation.10 | convolution fusion | flops 15043395584 | bytes 34078720 | tf_op jit(solution)/shard_map/dot_general | solution.py:173
  282.1 19.4 %fusion.6 = bf16[1024,4096]{1,0:T(8,128)(2,1)} fusion(bf16[1024,1792]{1,0:T(8,128)(2,1)} %multiply_convert_fusion, bf16[1,1792,4096]{2,1,0:T(8,128)(2,1)S(1)} %bitcast.160), kind=kOutput, calls=%fused_computation.9 | convolution fusion | flops 15036579840 | bytes 26738688 | tf_op jit(solution)/shard_map/dot_general | solution.py:175
  301.5 71.4 %reduce-scatter.5.cloned.1.call-done = bf16[1024,512]{1,0:T(8,128)(2,1)} async-done(((bf16[1024,4096]{1,0:T(8,128)(2,1)}), bf16[1024,512]{1,0:T(8,128)(2,1)}) %reduce-scatter.5.cloned.1.call-update) | async-done | bytes 1048592 | tf_op jit(solution)/shard_map/reduce_scatter | solution.py:176
  372.9 5.1 %all-to-all-start.3 = ((bf16[4,256,512]{2,1,0:T(8,128)(2,1)}), bf16[4,256,512]{2,1,0:T(8,128)(2,1)S(1)}, u32[]{:S(2)}, u32[]{:S(2)}) async-start(bf16[4,256,512]{2,1,0:T(8,128)(2,1)} %bitcast.147), calls=%async_computation.5 | async-start | bytes 2097152 | tf_op jit(solution)/shard_map/all_to_all | solution.py:179
  378.1 22.4 %all-to-all-done.3 = bf16[4,256,512]{2,1,0:T(8,128)(2,1)S(1)} async-done(((bf16[4,256,512]{2,1,0:T(8,128)(2,1)}), bf16[4,256,512]{2,1,0:T(8,128)(2,1)S(1)}, u32[]{:S(2)}, u32[]{:S(2)}) %all-to-all-start.3) | async-done | bytes 1048608 | tf_op jit(solution)/shard_map/all_to_all | solution.py:179
  400.5 2.0 gather_fusion.1
  402.5 0.7 reshape.270
  403.2 0.8 fusion.71
  404.0 0.9 fusion.34
  (63 shorter events, 1.5 us)
Async XLA Ops:
  6.5 43.0 %copy-start = (bf16[2,128,8,128]{3,2,1,0:T(8,128)(2,1)S(1)}, bf16[2,128,8,128]{3,2,1,0:T(8,128)(2,1)}, u32[]{:S(2)}) copy-start(bf16[2,128,8,128]{3,2,1,0:T(8,128)(2,1)} %param.18) | copy-start | bytes 1572868
  6.5 31.8 %all-gather.3.cloned.1.call-start = ((), (), s32[]{:S(2)}) async-start(), calls=%async_computation.6 | async-start | bytes 2359296 | tf_op jit(solution)/shard_map/all_gather | solution.py:60
  40.9 1.9 copy-start.2
  46.2 9.2 %all-to-all-start = ((bf16[8,2,512]{2,1,0:T(2,128)(2,1)}), bf16[8,2,512]{2,1,0:T(2,128)(2,1)S(1)}, u32[]{:S(2)}, u32[]{:S(2)}) async-start(bf16[8,2,512]{2,1,0:T(2,128)(2,1)} %reshape.304), calls=%async_computation | async-start | bytes 32768 | tf_op jit(solution)/shard_map/all_to_all | solution.py:81
  53.7 5.8 %copy-start.3 = (bf16[256,8,128]{2,1,0:T(8,128)(2,1)S(1)}, bf16[256,8,128]{2,1,0:T(8,128)(2,1)}, u32[]{:S(2)}) copy-start(bf16[256,8,128]{2,1,0:T(8,128)(2,1)} %param.16) | copy-start | bytes 1572868
  55.3 30.8 %all-to-all-start.1 = ((bf16[1,256,32,128]{3,1,0,2:T(8,128)(2,1)}), bf16[1,256,32,128]{3,1,0,2:T(8,128)(2,1)S(1)}, u32[]{:S(2)}, u32[]{:S(2)}) async-start(bf16[1,256,32,128]{3,1,0,2:T(8,128)(2,1)} %bitcast.142), calls=%async_computation.1 | async-start | bytes 4194304 | tf_op jit(solution)/shard_map/all_to_all | solution.py:74
  59.4 74.5 %reduce-scatter.3.cloned.1.call-start = ((), (), s32[]{:S(2)}) async-start(), calls=%async_computation.7 | async-start | bytes 2359296 | tf_op jit(solution)/shard_map/reduce_scatter | solution.py:131
  88.5 5.0 %copy-start.5 = (s32[256,2]{0,1:T(2,128)S(1)}, s32[256,2]{0,1:T(2,128)}, u32[]{:S(2)}) copy-start(s32[256,2]{0,1:T(2,128)} %param.24) | copy-start | bytes 6148
  88.6 45.4 %copy-start.4 = (bf16[256,512]{1,0:T(8,128)(2,1)S(1)}, bf16[256,512]{1,0:T(8,128)(2,1)}, u32[]{:S(2)}) copy-start(bf16[256,512]{1,0:T(8,128)(2,1)} %param.20) | copy-start | bytes 786436
  93.5 143.3 %all-gather.5.cloned.1.call-start = ((), (), s32[]{:S(2)}) async-start(), calls=%async_computation.8 | async-start | bytes 9437184 | tf_op jit(solution)/shard_map/all_gather | solution.py:169
  181.4 191.6 %reduce-scatter.5.cloned.1.call-start = ((), (), s32[]{:S(2)}) async-start(), calls=%async_computation.9 | async-start | bytes 9437184 | tf_op jit(solution)/shard_map/reduce_scatter | solution.py:176
  236.8 45.3 %slice-start = ((s8[14680064]{0:T(1024)(128)(4,1)}), s8[4194304]{0:T(1024)(128)(4,1)S(1)}, s32[]{:S(2)}) async-start(s8[14680064]{0:T(1024)(128)(4,1)} %bitcast.159), calls=%async_computation.10 | async-start | bytes 8388608
  236.8 45.3 %slice-start.1 = ((s8[14680064]{0:T(1024)(128)(4,1)}), s8[4194304]{0:T(1024)(128)(4,1)S(1)}, s32[]{:S(2)}) async-start(s8[14680064]{0:T(1024)(128)(4,1)} %bitcast.159), calls=%async_computation.11 | async-start | bytes 8388608
  258.6 23.5 %slice-start.2 = ((s8[14680064]{0:T(1024)(128)(4,1)}), s8[4194304]{0:T(1024)(128)(4,1)S(1)}, s32[]{:S(2)}) async-start(s8[14680064]{0:T(1024)(128)(4,1)} %bitcast.159), calls=%async_computation.12 | async-start | bytes 8388608
  258.6 23.5 %slice-start.3 = ((s8[14680064]{0:T(1024)(128)(4,1)}), s8[2097152]{0:T(1024)(128)(4,1)S(1)}, s32[]{:S(2)}) async-start(s8[14680064]{0:T(1024)(128)(4,1)} %bitcast.159), calls=%async_computation.13 | async-start | bytes 4194304
  372.9 27.6 %all-to-all-start.3 = ((bf16[4,256,512]{2,1,0:T(8,128)(2,1)}), bf16[4,256,512]{2,1,0:T(8,128)(2,1)S(1)}, u32[]{:S(2)}, u32[]{:S(2)}) async-start(bf16[4,256,512]{2,1,0:T(8,128)(2,1)} %bitcast.147), calls=%async_computation.5 | async-start | bytes 2097152 | tf_op jit(solution)/shard_map/all_to_all | solution.py:179
  400.5 4.3 %copy-start.1 = (bf16[2,128,8,128]{3,2,1,0:T(8,128)(2,1)S(1)}, bf16[2,128,8,128]{3,2,1,0:T(8,128)(2,1)}, u32[]{:S(2)}) copy-start(bf16[2,128,8,128]{3,2,1,0:T(8,128)(2,1)} %param.18) | copy-start | bytes 1572868
Sparse Core Ops, SparseCore 0:
  9.2 29.0 all-gather.2
  93.6 40.3 reduce-scatter.2
  181.5 55.2 all-gather.4
  301.6 71.2 reduce-scatter.4
where the time goes:
time: 416 us; the launch traced here: 411 us
  waiting for transfers between devices  236 us (57%)
  matrix products  80.7 us (19%)
  blocking collectives  41.1 us (10%)
  local copies, waits for them, and re-layouts  17.7 us (4%)
  between operations  13.5 us (3%)
  starting transfers between devices  12.9 us (3%)
  other arithmetic  9.78 us (2%)
    reduce_scatter x1, waiting for transfers between devices, per_device(): lax.psum_scatter(expert_partial.astype(jnp.bfloat16), 'tp', scatter_dimen...  71.4 us
    all_gather x1, waiting for transfers between devices, per_device(): fragment = lax.all_gather(incoming, 'tp', axis=2, tiled=True)  55.2 us
    reduce_scatter x1, waiting for transfers between devices, per_device(): lax.psum_scatter(head_partial.astype(jnp.bfloat16), 'tp', scatter_dimensi...  34.6 us
    all_to_all x1, blocking collectives, per_device(): lax.all_to_all(outgoing, 'req', split_axis=0, concat_axis=0, tiled=True)  28.1 us
    all_gather x1, waiting for transfers between devices, per_device(): every_query = lax.all_gather(queries, 'tp', axis=1, tiled=True)  26.5 us
    all_to_all x1, waiting for transfers between devices, per_device(): lax.all_to_all(far_mixture.reshape(1, local_rows, head_count, head_width)...  25.6 us
    dot_general x1, matrix products, per_device(): up_sums = jnp.dot(rows_in, up_matrix, preferred_element_type=jnp.float32)  23.5 us
    all_to_all x1, waiting for transfers between devices, per_device(): lax.all_to_all(expert_result.reshape(expert_devices, capacity, slice_widt...  22.4 us
  transfers between devices with their start and end apart: 7, of which 6 were waited for; matrix products, arithmetic and copies ran while one was open for 4% of the time, Pallas kernels for 0%

commit v1 on v0

v1 whole, which is shorter than its diff:
```python
import functools
import jax
import jax.numpy as jnp
from jax import lax
from jax.experimental import pallas as pl
from jax.experimental.pallas import tpu as pltpu
from jax.sharding import PartitionSpec as P

norm_eps = 1e-05
masked_score = -1e30
bf16 = jnp.bfloat16
f32 = jnp.float32
MIB = 1 << 20
unit_block = 512


def xor_swap(x, axis, mask):
    size = lax.axis_size(axis)
    return lax.ppermute(x, axis, [(i, i ^ mask) for i in range(size)])


def attend_kernel(devices, groups, scaling, lengths_ref, rank_ref, *refs):
    cached_ref, q_ref, kn_ref, vn_ref, ow_hbm, like_ref, other_ref, ow_ref, semaphore = refs
    fetch = pltpu.make_async_copy(ow_hbm, ow_ref, semaphore)

    @pl.when(pl.program_id(0) == 0)
    def _():
        fetch.start()

    rank = rank_ref[0]
    length = lengths_ref[pl.program_id(0)]
    key_heads, new_rows, width = kn_ref.shape
    span = cached_ref.shape[4]
    columns = like_ref.shape[2]
    cached = devices * span
    column = lax.broadcasted_iota(jnp.int32, (new_rows, cached), 1)
    far_bias = jnp.where(column < length, 0.0, masked_score)
    row = lax.broadcasted_iota(jnp.int32, (new_rows, new_rows), 0)
    step = lax.broadcasted_iota(jnp.int32, (new_rows, new_rows), 1)
    near_bias = jnp.where(step <= row, 0.0, masked_score)
    bias = jnp.concatenate([far_bias, near_bias], axis=1)
    outs = []
    for head in range(key_heads):
        keys = jnp.concatenate([cached_ref[d, head, 0, 0] for d in range(devices)] + [kn_ref[head]], axis=0)
        values = jnp.concatenate([cached_ref[d, head, 1, 0] for d in range(devices)] + [vn_ref[head]], axis=0)
        for g in range(groups):
            q = q_ref[head * groups + g]
            scores = (
                lax.dot_general(q, keys, (((1,), (1,)), ((), ())), preferred_element_type=f32)
                * scaling
            )
            scores = jnp.where(bias < 0.0, masked_score, scores)
            highest = jnp.max(scores, axis=1, keepdims=True)
            weights = jnp.exp(scores - highest)
            total = jnp.sum(weights, axis=1, keepdims=True)
            mixed = jnp.dot(weights.astype(bf16), values, preferred_element_type=f32)
            outs.append((mixed / total).astype(bf16))
    attention = jnp.concatenate(outs, axis=1)

    @pl.when(pl.program_id(0) == 0)
    def _():
        fetch.wait()

    for target, parity in ((like_ref, 0), (other_ref, 1)):
        for i in range(devices // 2):
            first = pl.multiple_of((rank ^ (2 * i + parity)) * columns, columns)
            term = jnp.dot(attention, ow_ref[:, pl.ds(first, columns)], preferred_element_type=f32)
            target[i] = term.astype(bf16)


def attend(lengths, rank, cached, q, kn, vn, out_weight, scaling):
    devices, key_heads, _, requests, span, width = cached.shape
    heads, rows, _ = q.shape
    new_rows = rows // requests
    model = out_weight.shape[1]
    columns = model // devices
    cached_spec = pl.BlockSpec(
        (devices, key_heads, 2, 1, span, width), lambda r, *_: (0, 0, 0, r, 0, 0)
    )
    near_spec = pl.BlockSpec((key_heads, new_rows, width), lambda r, *_: (0, r, 0))
    out_spec = pl.BlockSpec((devices // 2, new_rows, columns), lambda r, *_: (0, r, 0))
    out_type = jax.ShapeDtypeStruct((devices // 2, rows, columns), bf16)
    flops = 4 * rows * heads * width * (devices * span + new_rows) + 2 * rows * heads * width * model
    return pl.pallas_call(
        functools.partial(attend_kernel, devices, heads // key_heads, scaling),
        grid_spec=pltpu.PrefetchScalarGridSpec(
            num_scalar_prefetch=2,
            grid=(requests,),
            in_specs=[
                cached_spec,
                pl.BlockSpec((heads, new_rows, width), lambda r, *_: (0, r, 0)),
                near_spec,
                near_spec,
                pl.BlockSpec(memory_space=pl.ANY),
            ],
            out_specs=[out_spec, out_spec],
            scratch_shapes=[pltpu.VMEM(out_weight.shape, bf16), pltpu.SemaphoreType.DMA],
        ),
        out_shape=[out_type, out_type],
        compiler_params=pltpu.CompilerParams(vmem_limit_bytes=58 * MIB),
        cost_estimate=pl.CostEstimate(
            flops=flops, bytes_accessed=8 * MIB, transcendentals=rows * heads * devices * span
        ),
        name="attend",
    )(lengths, rank, cached, q, kn, vn, out_weight)


def blocks_of(size, block):
    return [(first, min(block, size - first)) for first in range(0, size, block)]


def units_kernel(devices, experts, scalars_ref, *refs):
    like_ref, other_ref, gain_ref, router_ref, routes_ref = refs[:5]
    gate_hbm, up_hbm, down_hbm, active_ref, weight_ref, odd_ref, down_ref = refs[5:12]
    normed_ref, gate_ref, up_ref, down_odd_ref, semaphores = refs[12:]
    spans = blocks_of(active_ref.shape[1], unit_block)
    count = len(spans)

    def fetch(n):
        first, size = spans[n]
        copies = [
            pltpu.make_async_copy(
                source.at[:, pl.ds(first, size)],
                target.at[n % 2, :, pl.ds(0, size)],
                semaphores.at[2 * n + i],
            )
            for i, (source, target) in enumerate(((gate_hbm, gate_ref), (up_hbm, up_ref)))
        ]
        for copy in copies:
            copy.start()
        return copies

    rank, expert = scalars_ref[0], scalars_ref[1]
    half, rows, columns = like_ref.shape
    model = devices * columns

    def fetch_down(n):
        parity, i = (1, n) if n < half else (0, n - half)
        first = pl.multiple_of((rank ^ (2 * i + parity)) * columns, columns)
        target = (down_odd_ref if parity else down_ref).at[i]
        copy = pltpu.make_async_copy(down_hbm.at[:, pl.ds(first, columns)], target, semaphores.at[2 * count + n])
        copy.start()
        return copy

    fetched, downs = [fetch(0)], []

    pieces = []
    for ref, parity in ((like_ref, 0), (other_ref, 1)):
        pieces += [(ref, i, rank ^ (2 * i + parity)) for i in range(devices // 2)]
    squares = jnp.zeros((rows, 1), f32)
    raw = jnp.zeros((rows, router_ref.shape[1]), f32)
    for ref, i, device in pieces:
        first = pl.multiple_of(device * columns, columns)
        value = ref[i].astype(f32)
        squares += jnp.sum(value * value, axis=1, keepdims=True)
        raw += jnp.dot(ref[i], router_ref[pl.ds(first, columns), :], preferred_element_type=f32)
    inverse = lax.rsqrt(squares / model + norm_eps)
    for ref, i, device in pieces:
        first = pl.multiple_of(device * columns, columns)
        value = ref[i].astype(f32) * inverse * gain_ref[device]
        normed_ref[:, pl.ds(first, columns)] = value.astype(bf16)
    logits = raw * inverse
    routes = routes_ref[...]
    one, two = routes[:, 0:1], routes[:, 1:2]
    lane = lax.broadcasted_iota(jnp.int32, raw.shape, 1)
    lane = jnp.where(lane < experts, lane, lane - experts)
    own_logit = jnp.sum(jnp.where(lane == expert, logits, 0.0), axis=1, keepdims=True)
    other_logit = jnp.sum(jnp.where(lane == one + two - expert, logits, 0.0), axis=1, keepdims=True)
    named = (one == expert) | (two == expert)
    weight = jnp.where(named, 1.0 / (1.0 + jnp.exp(other_logit - own_logit)), 0.0)
    weight_ref[...] = jnp.broadcast_to(weight, weight_ref.shape)

    for n, (first, size) in enumerate(spans):
        if n + 1 < count:
            fetched.append(fetch(n + 1))
        downs += [fetch_down(m) for m in range(len(downs), 2 * half * (n + 1) // (count + 1))]
        for copy in fetched[n]:
            copy.wait()
        block = n % 2, slice(None), pl.ds(0, size)
        gate = jnp.dot(normed_ref[...], gate_ref[block], preferred_element_type=f32)
        up = jnp.dot(normed_ref[...], up_ref[block], preferred_element_type=f32)
        active_ref[:, pl.ds(first, size)] = (gate / (1.0 + jnp.exp(-gate)) * up).astype(bf16)
    downs += [fetch_down(m) for m in range(len(downs), 2 * half)]
    for i in range(half):
        downs[i].wait()
        total = jnp.dot(active_ref[...], down_odd_ref[i], preferred_element_type=f32)
        odd_ref[i] = (total * weight_ref[:, 0:1]).astype(bf16)
    for copy in downs[half:]:
        copy.wait()


def run_units(experts, scalars, like, other, gain, router, routes, weights):
    half, rows, columns = like.shape
    model, units = weights[0].shape
    in_vmem = pl.BlockSpec(memory_space=pltpu.VMEM)
    in_hbm = pl.BlockSpec(memory_space=pl.ANY)
    out_shape = [jax.ShapeDtypeStruct((rows, units), bf16), jax.ShapeDtypeStruct((rows, 128), f32)]
    out_shape.append(jax.ShapeDtypeStruct((half, rows, columns), bf16))
    out_shape.append(pltpu.VMEM((half, units, columns), bf16))
    block = min(unit_block, units)
    return pl.pallas_call(
        functools.partial(units_kernel, 2 * half, experts),
        in_specs=[pl.BlockSpec(memory_space=pltpu.SMEM)] + [in_vmem] * 5 + [in_hbm] * len(weights),
        out_specs=[in_vmem] * len(out_shape),
        out_shape=out_shape,
        scratch_shapes=[
            pltpu.VMEM((rows, model), bf16),
            pltpu.VMEM((2, model, block), bf16),
            pltpu.VMEM((2, model, block), bf16),
            pltpu.VMEM((half, units, columns), bf16),
            pltpu.SemaphoreType.DMA((2 * len(blocks_of(units, block)) + 2 * half,)),
        ],
        compiler_params=pltpu.CompilerParams(vmem_limit_bytes=38 * MIB),
        cost_estimate=pl.CostEstimate(
            flops=4 * rows * model * units, bytes_accessed=6 * model * units, transcendentals=rows * units
        ),
        name="units",
    )(scalars, like, other, gain, router, routes, *weights)


def down_kernel(active_ref, weight_ref, down_ref, out_ref):
    for i in range(out_ref.shape[0]):
        total = jnp.dot(active_ref[...], down_ref[i], preferred_element_type=f32)
        out_ref[i] = (total * weight_ref[:, 0:1]).astype(bf16)


def run_down(active, weight, down):
    rows = active.shape[0]
    half, units, columns = down.shape
    in_vmem = pl.BlockSpec(memory_space=pltpu.VMEM)
    return pl.pallas_call(
        down_kernel,
        in_specs=[in_vmem] * 3,
        out_specs=in_vmem,
        out_shape=jax.ShapeDtypeStruct((half, rows, columns), bf16),
        compiler_params=pltpu.CompilerParams(vmem_limit_bytes=8 * MIB),
        cost_estimate=pl.CostEstimate(
            flops=2 * rows * down.size, bytes_accessed=2 * down.size, transcendentals=0
        ),
        name="down",
    )(active, weight, down)


def fence(*values):
    return lax.optimization_barrier(values)


def between_chips(piece):
    devices = lax.axis_size("tp")
    return [piece] + [xor_swap(piece, "tp", j) for j in range(2, devices, 2)]


def core_sums(like, arrived):
    return [
        (like[i].astype(f32) + arrived[i].astype(f32)).astype(bf16) for i in range(like.shape[0])
    ]


def scatter_chips(sums):
    return [sums[0]] + [xor_swap(x, "tp", 2 * i) for i, x in enumerate(sums) if i > 0]


def add_up(parts):
    total = parts[0].astype(f32)
    for x in parts[1:]:
        total += x.astype(f32)
    return total


def per_device(
    queries,
    key_new,
    value_new,
    cache_keys,
    cache_values,
    context_lengths,
    residual,
    out_weight,
    norm_gain,
    router,
    routes,
    gate_weight,
    up_weight,
    down_weight,
):
    devices = lax.axis_size("tp")
    planes = lax.axis_size("req")
    rank = lax.axis_index("tp")
    plane = lax.axis_index("req")
    heads, width = queries.shape[1], queries.shape[2]
    key_heads = cache_keys.shape[2]
    grouping = heads * devices // key_heads
    own_keys = max(1, heads // grouping)
    model = out_weight.shape[1]
    columns = model // devices

    cache = jnp.stack([cache_keys, cache_values]).transpose(3, 0, 1, 2, 4)
    if own_keys * devices != key_heads:
        cache = jnp.repeat(cache, own_keys * devices // key_heads, axis=0)
    cache = cache.reshape(devices, own_keys, *cache.shape[1:])
    cached = lax.all_to_all(cache, "tp", split_axis=0, concat_axis=0, tiled=True)
    first_key = rank * heads // grouping
    kn = lax.dynamic_slice_in_dim(key_new, first_key, own_keys, 1).transpose(1, 0, 2)
    vn = lax.dynamic_slice_in_dim(value_new, first_key, own_keys, 1).transpose(1, 0, 2)
    q = queries.transpose(1, 0, 2)
    gain = norm_gain.astype(f32)
    routing = gain[:, None] * router.astype(f32)
    high = routing.astype(bf16)
    low = (routing - high.astype(f32)).astype(bf16)
    routing = jnp.concatenate([high, low], axis=1)
    routing = jnp.pad(routing, ((0, 0), (0, -routing.shape[1] % 128)))
    gain = gain.reshape(devices, 1, columns)
    scalars = jnp.stack([rank, plane]).astype(jnp.int32)
    cached, routing, gain, scalars, q, kn, vn = fence(cached, routing, gain, scalars, q, kn, vn)

    like, other = attend(
        context_lengths, scalars[:1], cached, q, kn, vn, out_weight, width**-0.5
    )
    sums = core_sums(like, xor_swap(other, "tp", 1))
    sums, own_routes = fence(sums, routes)
    parts = scatter_chips(sums)
    chunk_routes = [own_routes] + [xor_swap(own_routes, "req", k) for k in range(1, planes)]
    parts, chunk_routes = fence(parts, chunk_routes)
    hidden = (residual.astype(f32) + add_up(parts)).astype(bf16)

    groups = [[0]] + [list(range(k, min(k + 2, planes))) for k in range(1, planes, 2)]
    half = devices // 2
    span = hidden.shape[0]
    weights = [gate_weight[0], up_weight[0], down_weight[0]]

    def joined(arrays, group):
        return arrays[group[0]] if len(group) == 1 else jnp.concatenate([arrays[k] for k in group], axis=0)

    def rows_of(near):
        rows = jnp.stack(near)
        return rows, xor_swap(rows, "tp", 1)

    near = between_chips(hidden)
    pieces = {k: xor_swap(hidden, "req", k) for k in range(1, min(planes, 3))}
    near, pieces, own = fence(near, pieces, hidden)
    pieces |= {k: xor_swap(own, "req", k) for k in range(3, planes)}
    like, other = rows_of(near)
    spread, back = {}, {}

    def send_back():
        for at in list(spread):
            total = add_up(spread.pop(at))
            for i, k in enumerate(groups[at]):
                part = total[i * span : (i + 1) * span]
                back[k] = xor_swap(part.astype(bf16), "req", k) if k else part

    for at, group in enumerate(groups):
        following = groups[at + 1] if at + 1 < len(groups) else None
        near = between_chips(joined(pieces, following)) if following else []
        active, weight, odd, down = run_units(
            planes, scalars, like, other, gain, routing, joined(chunk_routes, group), weights
        )
        near, spread, pieces, active, weight, odd, down = fence(
            near, spread, pieces, active, weight, odd, down
        )
        if following:
            like, other = rows_of(near)
        send_back()
        arrived = xor_swap(odd, "tp", 1)
        even = run_down(active, weight, down)
        even, arrived, other, pieces = fence(even, arrived, other, pieces)
        spread[at] = scatter_chips(core_sums(even, arrived))
    send_back()
    total = hidden.astype(f32)
    for k in range(planes):
        total += back[k].astype(f32)
    return total.astype(bf16)


def solution(mesh):
    placed = (
        P("req", "tp", None),
        P("req", None, None),
        P("req", None, None),
        P("req", "tp", None, None),
        P("req", "tp", None, None),
        P("req"),
        P("req", "tp"),
        P("tp", None),
        P(),
        P(),
        P("req", None),
        P("req", None, "tp"),
        P("req", None, "tp"),
        P("req", "tp", None),
    )
    return jax.shard_map(
        per_device, mesh=mesh, in_specs=placed, out_specs=P("req", "tp"), check_vma=False
    )
```

time: 416 us -> 216 us (0.52)
  waiting for transfers between devices: 236 us -> 70.8 us
  Pallas kernels: 0 us -> 83 us
  matrix products: 80.7 us -> 0 us
  blocking collectives: 41.1 us -> 0 us
  starting transfers between devices: 12.9 us -> 39.4 us
  between operations: 13.5 us -> 0.92 us
  local copies, waits for them, and re-layouts: 17.7 us -> 9.69 us
    reduce_scatter x2 -> x0, waiting for transfers between devices: 106 us -> none  [the longest x1 71.4 us: per_device(): lax.psum_scatter(expert_partial.astype(jnp.bfloat16), 'tp', scatter_dimen...]
    pallas_call x0 -> x7, Pallas kernels: none -> 83 us  [the longest x3 65.6 us: run_units(): pl.pallas_call(functools.partial(units_kernel, 2 * half, experts), in_spe...]
    all_gather x2 -> x0, waiting for transfers between devices: 81.6 us -> none  [the longest x1 55.2 us: per_device(): fragment = lax.all_gather(incoming, 'tp', axis=2, tiled=True)]
    dot_general x11 -> x0, matrix products: 80.7 us -> none  [the longest x1 23.5 us: per_device(): up_sums = jnp.dot(rows_in, up_matrix, preferred_element_type=jnp.float32)]
    ppermute x0 -> x37, waiting for transfers between devices: none -> 60.3 us  [xor_swap(): return lax.ppermute(x, axis, [(i, i ^ mask) for i in range(size)])]
    all_to_all x3 -> x1, waiting for transfers between devices: 48 us -> 10.4 us  [per_device(): lax.all_to_all(cache, 'tp', split_axis=0, concat_axis=0, tiled=True)]
    ppermute x0 -> x37, starting transfers between devices: none -> 35.5 us  [xor_swap(): return lax.ppermute(x, axis, [(i, i ^ mask) for i in range(size)])]
    all_to_all x1 -> x0, blocking collectives: 28.1 us -> none  [per_device(): lax.all_to_all(outgoing, 'req', split_axis=0, concat_axis=0, tiled=True)]
  transfers between devices with their start and end apart: 7 -> 38, of which waited for: 6 -> 18; matrix products, arithmetic and copies ran while one was open for 4% -> 4% of each run, Pallas kernels for 0% -> 35%
where the time goes in v1:
time: 216 us; the launch traced here: 213 us
  Pallas kernels  83 us (38%)
  waiting for transfers between devices  70.8 us (33%)
  starting transfers between devices  39.4 us (18%)
  local copies, waits for them, and re-layouts  9.69 us (4%)
  other arithmetic  8.69 us (4%)
    pallas_call x3, Pallas kernels, run_units(): pl.pallas_call(functools.partial(units_kernel, 2 * half, experts), in_spe...  65.6 us
    ppermute x37, waiting for transfers between devices, xor_swap(): return lax.ppermute(x, axis, [(i, i ^ mask) for i in range(size)])  60.3 us
    ppermute x37, starting transfers between devices, xor_swap(): return lax.ppermute(x, axis, [(i, i ^ mask) for i in range(size)])  35.5 us
    all_to_all x1, waiting for transfers between devices, per_device(): lax.all_to_all(cache, 'tp', split_axis=0, concat_axis=0, tiled=True)  10.4 us
    pallas_call x1, Pallas kernels, attend(): pl.pallas_call(functools.partial(attend_kernel, devices, heads // key_hea...  9.22 us
    pallas_call x3, Pallas kernels, run_down(): pl.pallas_call(down_kernel, in_specs=[in_vmem] * 3, out_specs=in_vmem, ou...  8.25 us
    unnamed x44, local copies, waits for them, and re-layouts  4.69 us
  transfers between devices with their start and end apart: 38, of which 18 were waited for; matrix products, arithmetic and copies ran while one was open for 4% of the time, Pallas kernels for 35%

profile of v1, /device:TPU:8, one launch (start us, length us, event | category | flops | bytes accessed | tf_op | source)
XLA Modules:
  0.0 212.5 jit_solution(9313283458584303899)
XLA Ops:
  0.0 1.4 copy_bitcast_fusion
  1.5 1.1 maximum_bitcast_fusion
  2.6 3.9 %all-to-all-start = ((bf16[8,1,2,2,128,128]{5,4,3,2,1,0:T(8,128)(2,1)}), bf16[8,1,2,2,128,128]{5,4,3,2,1,0:T(8,128)(2,1)S(1)}, u32[]{:S(2)}, u32[]{:S(2)}) async-start(bf16[8,1,2,2,128,128]{5,4,3,2,1,0:T(8,128)(2,1)} %maximum_bitcast_fusion), calls=%async_computation | async-start | bytes 2097152 | tf_op jit(solution)/shard_map/all_to_all | solution.py:301
  6.5 1.5 constant_dynamic-slice_fusion
  11.4 10.4 %all-to-all-done.refs_0_ = bf16[8,1,2,2,128,128]{5,4,3,2,1,0:T(8,128)(2,1)S(1)} async-done(((bf16[8,1,2,2,128,128]{5,4,3,2,1,0:T(8,128)(2,1)}), bf16[8,1,2,2,128,128]{5,4,3,2,1,0:T(8,128)(2,1)S(1)}, u32[]{:S(2)}, u32[]{:S(2)}) %all-to-all-start) | async-done | bytes 1048608 | tf_op jit(solution)/shard_map/all_to_all | solution.py:301
  21.9 1.0 copy-done.7
  22.9 9.2 %attend.1 = (bf16[4,256,512]{2,1,0:T(8,128)(2,1)}, bf16[4,256,512]{2,1,0:T(8,128)(2,1)}) custom-call(s32[2]{0:T(128)} %lengths_ref.1, s32[1]{0:T(128)} %bitcast.74, bf16[8,1,2,2,128,128]{5,4,3,2,1,0:T(8,128)(2,1)} %copy-done.7, bf16[4,256,128]{2,1,0:T(8,128)(2,1)} %bitcast.89, bf16[1,256,128]{2,1,0:T(8,128)(2,1)} %bitcast.98, bf16[1,256,128]{2,1,0:T(8,128)(2,1)} %bitcast.97, ...), custom_call_target="tpu_custom_call" | custom-call | flops 1677721600 | bytes 8388608 | tf_op jit(solution)/shard_map/attend/pallas_call | solution.py:84
  32.2 2.9 %collective-permute-done = bf16[4,256,512]{2,1,0:T(8,128)(2,1)S(1)} collective-permute-done((bf16[4,256,512]{2,1,0:T(8,128)(2,1)}, bf16[4,256,512]{2,1,0:T(8,128)(2,1)S(1)}, u32[]{:S(2)}, u32[]{:S(2)}) %collective-permute-start) | collective-permute-done | bytes 1048608 | tf_op jit(solution)/shard_map/ppermute | solution.py:19
  35.1 1.5 fusion.10
  37.8 2.3 %collective-permute-start.3 = (bf16[256,512]{1,0:T(8,128)(2,1)S(1)}, bf16[256,512]{1,0:T(8,128)(2,1)S(1)}, u32[]{:S(2)}, u32[]{:S(2)}) collective-permute-start(bf16[256,512]{1,0:T(8,128)(2,1)S(1)} %get-tuple-element.94), channel_id=1, source_target_pairs={{0,6},{1,7},{2,4},{3,5},{4,2},{5,3},{6,0},{7,1},{8,14},{9,15},{10,... | collective-permute-start | bytes 786440 | tf_op jit(solution)/shard_map/ppermute | solution.py:19
  40.1 2.6 %collective-permute-start.5 = (s32[256,2]{0,1:T(2,128)S(1)}, s32[256,2]{0,1:T(2,128)S(1)}, u32[]{:S(2)}, u32[]{:S(2)}) collective-permute-start(s32[256,2]{0,1:T(2,128)S(1)} %copy-done.17), channel_id=1, source_target_pairs={{0,16},{8,24},{16,0},{24,8},{1,17},{9,25},{17,1},{25,9},{2,18},{10... | collective-permute-start | bytes 6152 | tf_op jit(solution)/shard_map/ppermute | solution.py:19
  43.3 1.3 collective-permute-done.5
  44.6 1.6 collective-permute-start.6
  46.3 4.7 %collective-permute-done.6.refs_4_ = s32[256,2]{1,0:T(8,128)S(1)} collective-permute-done((s32[256,2]{1,0:T(8,128)S(1)}, s32[256,2]{1,0:T(8,128)S(1)}, u32[]{:S(2)}, u32[]{:S(2)}) %collective-permute-start.6) | collective-permute-done | bytes 2080 | tf_op jit(solution)/shard_map/ppermute | solution.py:19
  51.2 3.1 %collective-permute-start.11 = (bf16[256,512]{1,0:T(8,128)(2,1)S(1)}, bf16[256,512]{1,0:T(8,128)(2,1)S(1)}, u32[]{:S(2)}, u32[]{:S(2)}) collective-permute-start(bf16[256,512]{1,0:T(8,128)(2,1)S(1)} %add_convert_fusion.14), channel_id=1, source_target_pairs={{0,16},{8,24},{16,0},{24,8},{1,17},{9,25},{17,1},{25,9},{2,18},{10... | collective-permute-start | bytes 786440 | tf_op jit(solution)/shard_map/ppermute | solution.py:19
  54.3 1.4 collective-permute-start.9
  55.7 1.5 collective-permute-start.8
  57.8 6.3 %collective-permute-done.11 = bf16[256,512]{1,0:T(8,128)(2,1)S(1)} collective-permute-done((bf16[256,512]{1,0:T(8,128)(2,1)S(1)}, bf16[256,512]{1,0:T(8,128)(2,1)S(1)}, u32[]{:S(2)}, u32[]{:S(2)}) %collective-permute-start.11) | collective-permute-done | bytes 262176 | tf_op jit(solution)/shard_map/ppermute | solution.py:19
  64.0 1.1 collective-permute-done.10
  65.1 2.3 %collective-permute-done.8 = bf16[256,512]{1,0:T(8,128)(2,1)S(1)} collective-permute-done((bf16[256,512]{1,0:T(8,128)(2,1)S(1)}, bf16[256,512]{1,0:T(8,128)(2,1)S(1)}, u32[]{:S(2)}, u32[]{:S(2)}) %collective-permute-start.8) | collective-permute-done | bytes 262176 | tf_op jit(solution)/shard_map/ppermute | solution.py:19
  67.8 1.0 constant_dynamic-update-slice_fusion.1
  68.8 1.0 constant_dynamic-update-slice_fusion
  69.8 1.5 collective-permute-start.14
  71.9 1.4 collective-permute-start.12
  73.8 17.7 %units.3 = (bf16[256,1792]{1,0:T(8,128)(2,1)S(1)}, f32[256,128]{1,0:T(8,128)S(1)}, bf16[4,256,512]{2,1,0:T(8,128)(2,1)S(1)}, bf16[4,1792,512]{2,1,0:T(8,128)(2,1)S(1)}) custom-call(s32[2]{0:T(128)S(1)} %copy-done.2, bf16[4,256,512]{2,1,0:T(8,128)(2,1)S(1)} %pad_maximum_fusion.1.refs_0_, bf16[4,256,512]{2,1,0:T(8,128)(2,1)S(1)} %collective-permute-done.16.refs_1_, ...), custom_call_target="tpu_custom_call" | custom-call | flops 7516192768 | bytes 44040192 | tf_op jit(solution)/shard_map/units/pallas_call | solution.py:201
  91.5 4.7 %collective-permute-done.13 = bf16[512,512]{1,0:T(8,128)(2,1)S(1)} collective-permute-done((bf16[512,512]{1,0:T(8,128)(2,1)S(1)}, bf16[512,512]{1,0:T(8,128)(2,1)S(1)}, u32[]{:S(2)}, u32[]{:S(2)}) %collective-permute-start.13) | collective-permute-done | bytes 524320 | tf_op jit(solution)/shard_map/ppermute | solution.py:19
  97.1 2.2 %down.3 = bf16[4,256,512]{2,1,0:T(8,128)(2,1)S(1)} custom-call(bf16[256,1792]{1,0:T(8,128)(2,1)S(1)} %get-tuple-element.114.active_ref, f32[256,128]{1,0:T(8,128)S(1)} %get-tuple-element.115.weight_ref, bf16[4,1792,512]{2,1,0:T(8,128)(2,1)S(1)} %get-tuple-element.116.down_ref), custom_call_target="tpu_custom_call" | custom-call | flops 1879048192 | bytes 7340032 | tf_op jit(solution)/shard_map/down/pallas_call | solution.py:231
  99.4 2.9 %collective-permute-done.17 = bf16[4,256,512]{2,1,0:T(8,128)(2,1)S(1)} collective-permute-done((bf16[4,256,512]{2,1,0:T(8,128)(2,1)S(1)}, bf16[4,256,512]{2,1,0:T(8,128)(2,1)S(1)}, u32[]{:S(2)}, u32[]{:S(2)}) %collective-permute-start.17) | collective-permute-done | bytes 1048608 | tf_op jit(solution)/shard_map/ppermute | solution.py:19
  102.3 1.4 fusion.14
  103.7 1.4 collective-permute-start.24
  105.3 1.6 collective-permute-start.21
  107.8 1.1 collective-permute-start.19
  109.5 4.7 %collective-permute-done.24 = bf16[256,512]{1,0:T(8,128)(2,1)} collective-permute-done((bf16[256,512]{1,0:T(8,128)(2,1)}, bf16[256,512]{1,0:T(8,128)(2,1)}, u32[]{:S(2)}, u32[]{:S(2)}) %collective-permute-start.24) | collective-permute-done | bytes 262176 | tf_op jit(solution)/shard_map/ppermute | solution.py:19
  114.8 30.3 %units.4 = (bf16[512,1792]{1,0:T(8,128)(2,1)S(1)}, f32[512,128]{1,0:T(8,128)S(1)}, bf16[4,512,512]{2,1,0:T(8,128)(2,1)S(1)}, bf16[4,1792,512]{2,1,0:T(8,128)(2,1)S(1)}) custom-call(s32[2]{0:T(128)S(1)} %copy-done.3, bf16[4,512,512]{2,1,0:T(8,128)(2,1)S(1)} %pad_maximum_fusion.refs_0_, bf16[4,512,512]{2,1,0:T(8,128)(2,1)} %copy-done.19, ...), custom_call_target="tpu_custom_call" | custom-call | flops 15032385536 | bytes 44040192 | tf_op jit(solution)/shard_map/units/pallas_call | solution.py:201
  146.1 3.9 %down.4 = bf16[4,512,512]{2,1,0:T(8,128)(2,1)S(1)} custom-call(bf16[512,1792]{1,0:T(8,128)(2,1)S(1)} %get-tuple-element.137.active_ref, f32[512,128]{1,0:T(8,128)S(1)} %get-tuple-element.138.weight_ref, bf16[4,1792,512]{2,1,0:T(8,128)(2,1)S(1)} %get-tuple-element.139.down_ref), custom_call_target="tpu_custom_call" | custom-call | flops 3758096384 | bytes 7340032 | tf_op jit(solution)/shard_map/down/pallas_call | solution.py:231
  151.5 1.8 collective-permute-start.29
  153.4 1.1 collective-permute-start.28
  155.1 17.6 %units.5 = (bf16[256,1792]{1,0:T(8,128)(2,1)S(1)}, f32[256,128]{1,0:T(8,128)S(1)}, bf16[4,256,512]{2,1,0:T(8,128)(2,1)S(1)}, bf16[4,1792,512]{2,1,0:T(8,128)(2,1)S(1)}) custom-call(s32[2]{0:T(128)S(1)} %copy-done.3, bf16[4,256,512]{2,1,0:T(8,128)(2,1)S(1)} %pad_maximum_fusion.2.refs_0_, bf16[4,256,512]{2,1,0:T(8,128)(2,1)S(1)} %collective-permute-done.26.refs_1_, ...), custom_call_target="tpu_custom_call" | custom-call | flops 7516192768 | bytes 44040192 | tf_op jit(solution)/shard_map/units/pallas_call | solution.py:201
  172.7 5.0 %collective-permute-done.28 = bf16[512,512]{1,0:T(8,128)(2,1)S(1)} collective-permute-done((bf16[512,512]{1,0:T(8,128)(2,1)S(1)}, bf16[512,512]{1,0:T(8,128)(2,1)S(1)}, u32[]{:S(2)}, u32[]{:S(2)}) %collective-permute-start.28) | collective-permute-done | bytes 524320 | tf_op jit(solution)/shard_map/ppermute | solution.py:19
  177.7 2.1 down.5
  180.6 1.5 collective-permute-start.33
  182.1 1.4 collective-permute-start.35
  184.5 1.6 collective-permute-start.30
  186.5 3.3 %collective-permute-done.33 = bf16[256,512]{1,0:T(8,128)(2,1)S(1)} collective-permute-done((bf16[256,512]{1,0:T(8,128)(2,1)S(1)}, bf16[256,512]{1,0:T(8,128)(2,1)S(1)}, u32[]{:S(2)}, u32[]{:S(2)}) %collective-permute-start.33) | collective-permute-done | bytes 262176 | tf_op jit(solution)/shard_map/ppermute | solution.py:19
  189.8 5.7 %collective-permute-done.35 = bf16[256,512]{1,0:T(8,128)(2,1)S(1)} collective-permute-done((bf16[256,512]{1,0:T(8,128)(2,1)S(1)}, bf16[256,512]{1,0:T(8,128)(2,1)S(1)}, u32[]{:S(2)}, u32[]{:S(2)}) %collective-permute-start.35) | collective-permute-done | bytes 262176 | tf_op jit(solution)/shard_map/ppermute | solution.py:19
  195.5 1.4 collective-permute-done.34
  197.7 12.5 %collective-permute-done.36 = bf16[256,512]{1,0:T(8,128)(2,1)S(1)} collective-permute-done((bf16[256,512]{1,0:T(8,128)(2,1)S(1)}, bf16[256,512]{1,0:T(8,128)(2,1)S(1)}, u32[]{:S(2)}, u32[]{:S(2)}) %collective-permute-start.36) | collective-permute-done | bytes 262176 | tf_op jit(solution)/shard_map/ppermute | solution.py:19
  210.1 1.9 add_convert_fusion.5
  (105 shorter events, 16.9 us)
Async XLA Ops:
  2.6 19.3 %all-to-all-start = ((bf16[8,1,2,2,128,128]{5,4,3,2,1,0:T(8,128)(2,1)}), bf16[8,1,2,2,128,128]{5,4,3,2,1,0:T(8,128)(2,1)S(1)}, u32[]{:S(2)}, u32[]{:S(2)}) async-start(bf16[8,1,2,2,128,128]{5,4,3,2,1,0:T(8,128)(2,1)} %maximum_bitcast_fusion), calls=%async_computation | async-start | bytes 2097152 | tf_op jit(solution)/shard_map/all_to_all | solution.py:301
  32.1 8.0 %copy-start.17 = (s32[256,2]{0,1:T(2,128)S(1)}, s32[256,2]{0,1:T(2,128)}, u32[]{:S(2)}) copy-start(s32[256,2]{0,1:T(2,128)} %param.24) | copy-start | bytes 6148
  32.1 18.9 %copy-start.13 = (bf16[256,512]{1,0:T(8,128)(2,1)S(1)}, bf16[256,512]{1,0:T(8,128)(2,1)}, u32[]{:S(2)}) copy-start(bf16[256,512]{1,0:T(8,128)(2,1)} %param.20) | copy-start | bytes 786436
  32.2 2.9 %collective-permute-start = (bf16[4,256,512]{2,1,0:T(8,128)(2,1)}, bf16[4,256,512]{2,1,0:T(8,128)(2,1)S(1)}, u32[]{:S(2)}, u32[]{:S(2)}) collective-permute-start(bf16[4,256,512]{2,1,0:T(8,128)(2,1)} %get-tuple-element.90), channel_id=1, source_target_pairs={{0,1},{1,0},{2,3},{3,2},{4,5},{5,4},{6,7},{7,6},{8,9},{9,8},{10,11... | collective-permute-start | bytes 3145736 | tf_op jit(solution)/shard_map/ppermute | solution.py:19
  36.6 14.4 %collective-permute-start.1 = (bf16[256,512]{1,0:T(8,128)(2,1)S(1)}, bf16[256,512]{1,0:T(8,128)(2,1)S(1)}, u32[]{:S(2)}, u32[]{:S(2)}) collective-permute-start(bf16[256,512]{1,0:T(8,128)(2,1)S(1)} %get-tuple-element.92), channel_id=1, source_target_pairs={{0,2},{1,3},{2,0},{3,1},{4,6},{5,7},{6,4},{7,5},{8,10},{9,11},{10,... | collective-permute-start | bytes 786440 | tf_op jit(solution)/shard_map/ppermute | solution.py:19
  37.2 13.8 %collective-permute-start.2 = (bf16[256,512]{1,0:T(8,128)(2,1)S(1)}, bf16[256,512]{1,0:T(8,128)(2,1)S(1)}, u32[]{:S(2)}, u32[]{:S(2)}) collective-permute-start(bf16[256,512]{1,0:T(8,128)(2,1)S(1)} %get-tuple-element.93), channel_id=1, source_target_pairs={{0,4},{1,5},{2,6},{3,7},{4,0},{5,1},{6,2},{7,3},{8,12},{9,13},{10,... | collective-permute-start | bytes 786440 | tf_op jit(solution)/shard_map/ppermute | solution.py:19
  37.8 13.2 %collective-permute-start.3 = (bf16[256,512]{1,0:T(8,128)(2,1)S(1)}, bf16[256,512]{1,0:T(8,128)(2,1)S(1)}, u32[]{:S(2)}, u32[]{:S(2)}) collective-permute-start(bf16[256,512]{1,0:T(8,128)(2,1)S(1)} %get-tuple-element.94), channel_id=1, source_target_pairs={{0,6},{1,7},{2,4},{3,5},{4,2},{5,3},{6,0},{7,1},{8,14},{9,15},{10,... | collective-permute-start | bytes 786440 | tf_op jit(solution)/shard_map/ppermute | solution.py:19
  40.1 4.5 %collective-permute-start.5 = (s32[256,2]{0,1:T(2,128)S(1)}, s32[256,2]{0,1:T(2,128)S(1)}, u32[]{:S(2)}, u32[]{:S(2)}) collective-permute-start(s32[256,2]{0,1:T(2,128)S(1)} %copy-done.17), channel_id=1, source_target_pairs={{0,16},{8,24},{16,0},{24,8},{1,17},{9,25},{17,1},{25,9},{2,18},{10... | collective-permute-start | bytes 6152 | tf_op jit(solution)/shard_map/ppermute | solution.py:19
  42.7 3.6 %collective-permute-start.4 = (s32[256,2]{0,1:T(2,128)S(1)}, s32[256,2]{0,1:T(2,128)S(1)}, u32[]{:S(2)}, u32[]{:S(2)}) collective-permute-start(s32[256,2]{0,1:T(2,128)S(1)} %copy-done.17), channel_id=1, source_target_pairs={{0,8},{8,0},{16,24},{24,16},{1,9},{9,1},{17,25},{25,17},{2,10},{10... | collective-permute-start | bytes 6152 | tf_op jit(solution)/shard_map/ppermute | solution.py:19
  43.3 30.5 %copy-start.2 = (s32[2]{0:T(128)S(1)}, s32[2]{0:T(128)}, u32[]{:S(2)}) copy-start(s32[2]{0:T(128)} %pad_add_fusion.1.scalars_ref) | copy-start | bytes 28
  44.6 6.4 %collective-permute-start.6 = (s32[256,2]{1,0:T(8,128)S(1)}, s32[256,2]{1,0:T(8,128)S(1)}, u32[]{:S(2)}, u32[]{:S(2)}) collective-permute-start(s32[256,2]{1,0:T(8,128)S(1)} %copy.43), channel_id=1, source_target_pairs={{0,24},{8,16},{16,8},{24,0},{1,25},{9,17},{17,9},{25,1},{2,26},{10... | collective-permute-start | bytes 6152 | tf_op jit(solution)/shard_map/ppermute | solution.py:19
  51.0 16.4 %copy-start = (s32[256,2]{1,0:T(8,128)}, s32[256,2]{1,0:T(8,128)S(1)}, u32[]{:S(2)}) copy-start(s32[256,2]{1,0:T(8,128)S(1)} %collective-permute-done.6.refs_4_) | copy-start | bytes 6148
  51.2 16.4 %copy-start.4 = (bf16[256,512]{1,0:T(8,128)(2,1)}, bf16[256,512]{1,0:T(8,128)(2,1)S(1)}, u32[]{:S(2)}) copy-start(bf16[256,512]{1,0:T(8,128)(2,1)S(1)} %add_convert_fusion.14) | copy-start | bytes 786436
  51.2 12.8 %collective-permute-start.11 = (bf16[256,512]{1,0:T(8,128)(2,1)S(1)}, bf16[256,512]{1,0:T(8,128)(2,1)S(1)}, u32[]{:S(2)}, u32[]{:S(2)}) collective-permute-start(bf16[256,512]{1,0:T(8,128)(2,1)S(1)} %add_convert_fusion.14), channel_id=1, source_target_pairs={{0,16},{8,24},{16,0},{24,8},{1,17},{9,25},{17,1},{25,9},{2,18},{10... | collective-permute-start | bytes 786440 | tf_op jit(solution)/shard_map/ppermute | solution.py:19
  54.3 10.8 %collective-permute-start.10 = (bf16[256,512]{1,0:T(8,128)(2,1)S(1)}, bf16[256,512]{1,0:T(8,128)(2,1)S(1)}, u32[]{:S(2)}, u32[]{:S(2)}) collective-permute-start(bf16[256,512]{1,0:T(8,128)(2,1)S(1)} %add_convert_fusion.14), channel_id=1, source_target_pairs={{0,8},{8,0},{16,24},{24,16},{1,9},{9,1},{17,25},{25,17},{2,10},{10... | collective-permute-start | bytes 786440 | tf_op jit(solution)/shard_map/ppermute | solution.py:19
  54.3 10.8 %collective-permute-start.9 = (bf16[256,512]{1,0:T(8,128)(2,1)S(1)}, bf16[256,512]{1,0:T(8,128)(2,1)S(1)}, u32[]{:S(2)}, u32[]{:S(2)}) collective-permute-start(bf16[256,512]{1,0:T(8,128)(2,1)S(1)} %add_convert_fusion.14), channel_id=1, source_target_pairs={{0,6},{1,7},{2,4},{3,5},{4,2},{5,3},{6,0},{7,1},{8,14},{9,15},{10,... | collective-permute-start | bytes 786440 | tf_op jit(solution)/shard_map/ppermute | solution.py:19
  55.7 11.8 %collective-permute-start.8 = (bf16[256,512]{1,0:T(8,128)(2,1)S(1)}, bf16[256,512]{1,0:T(8,128)(2,1)S(1)}, u32[]{:S(2)}, u32[]{:S(2)}) collective-permute-start(bf16[256,512]{1,0:T(8,128)(2,1)S(1)} %add_convert_fusion.14), channel_id=1, source_target_pairs={{0,4},{1,5},{2,6},{3,7},{4,0},{5,1},{6,2},{7,3},{8,12},{9,13},{10,... | collective-permute-start | bytes 786440 | tf_op jit(solution)/shard_map/ppermute | solution.py:19
  57.1 10.3 %collective-permute-start.7 = (bf16[256,512]{1,0:T(8,128)(2,1)S(1)}, bf16[256,512]{1,0:T(8,128)(2,1)S(1)}, u32[]{:S(2)}, u32[]{:S(2)}) collective-permute-start(bf16[256,512]{1,0:T(8,128)(2,1)S(1)} %add_convert_fusion.14), channel_id=1, source_target_pairs={{0,2},{1,3},{2,0},{3,1},{4,6},{5,7},{6,4},{7,5},{8,10},{9,11},{10,... | collective-permute-start | bytes 786440 | tf_op jit(solution)/shard_map/ppermute | solution.py:19
  67.6 6.2 %collective-permute-start.16 = (bf16[4,256,512]{2,1,0:T(8,128)(2,1)S(1)}, bf16[4,256,512]{2,1,0:T(8,128)(2,1)S(1)}, u32[]{:S(2)}, u32[]{:S(2)}) collective-permute-start(bf16[4,256,512]{2,1,0:T(8,128)(2,1)S(1)} %pad_maximum_fusion.1.refs_0_), channel_id=1, source_target_pairs={{0,1},{1,0},{2,3},{3,2},{4,5},{5,4},{6,7},{7,6},{8,9},{9,8},{10,11... | collective-permute-start | bytes 3145736 | tf_op jit(solution)/shard_map/ppermute | solution.py:19
  69.8 21.8 %collective-permute-start.14 = (bf16[512,512]{1,0:T(8,128)(2,1)S(1)}, bf16[512,512]{1,0:T(8,128)(2,1)S(1)}, u32[]{:S(2)}, u32[]{:S(2)}) collective-permute-start(bf16[512,512]{1,0:T(8,128)(2,1)S(1)} %constant_dynamic-update-slice_fusion), channel_id=1, source_target_pairs={{0,6},{1,7},{2,4},{3,5},{4,2},{5,3},{6,0},{7,1},{8,14},{9,15},{10,... | collective-permute-start | bytes 1572872 | tf_op jit(solution)/shard_map/ppermute | solution.py:19
  71.2 25.0 %collective-permute-start.13 = (bf16[512,512]{1,0:T(8,128)(2,1)S(1)}, bf16[512,512]{1,0:T(8,128)(2,1)S(1)}, u32[]{:S(2)}, u32[]{:S(2)}) collective-permute-start(bf16[512,512]{1,0:T(8,128)(2,1)S(1)} %constant_dynamic-update-slice_fusion), channel_id=1, source_target_pairs={{0,4},{1,5},{2,6},{3,7},{4,0},{5,1},{6,2},{7,3},{8,12},{9,13},{10,... | collective-permute-start | bytes 1572872 | tf_op jit(solution)/shard_map/ppermute | solution.py:19
  71.9 24.4 %collective-permute-start.12 = (bf16[512,512]{1,0:T(8,128)(2,1)S(1)}, bf16[512,512]{1,0:T(8,128)(2,1)S(1)}, u32[]{:S(2)}, u32[]{:S(2)}) collective-permute-start(bf16[512,512]{1,0:T(8,128)(2,1)S(1)} %constant_dynamic-update-slice_fusion), channel_id=1, source_target_pairs={{0,2},{1,3},{2,0},{3,1},{4,6},{5,7},{6,4},{7,5},{8,10},{9,11},{10,... | collective-permute-start | bytes 1572872 | tf_op jit(solution)/shard_map/ppermute | solution.py:19
  73.3 18.2 %collective-permute-start.15 = (bf16[256,512]{1,0:T(8,128)(2,1)}, bf16[256,512]{1,0:T(8,128)(2,1)S(1)}, u32[]{:S(2)}, u32[]{:S(2)}) collective-permute-start(bf16[256,512]{1,0:T(8,128)(2,1)} %copy-done.4), channel_id=1, source_target_pairs={{0,24},{8,16},{16,8},{24,0},{1,25},{9,17},{17,9},{25,1},{2,26},{10... | collective-permute-start | bytes 786440 | tf_op jit(solution)/shard_map/ppermute | solution.py:19
  96.6 5.7 %collective-permute-start.18 = (bf16[4,512,512]{2,1,0:T(8,128)(2,1)S(1)}, bf16[4,512,512]{2,1,0:T(8,128)(2,1)S(1)}, u32[]{:S(2)}, u32[]{:S(2)}) collective-permute-start(bf16[4,512,512]{2,1,0:T(8,128)(2,1)S(1)} %pad_maximum_fusion.refs_0_), channel_id=1, source_target_pairs={{0,1},{1,0},{2,3},{3,2},{4,5},{5,4},{6,7},{7,6},{8,9},{9,8},{10,11... | collective-permute-start | bytes 6291464 | tf_op jit(solution)/shard_map/ppermute | solution.py:19
  96.7 5.6 %collective-permute-start.17 = (bf16[4,256,512]{2,1,0:T(8,128)(2,1)S(1)}, bf16[4,256,512]{2,1,0:T(8,128)(2,1)S(1)}, u32[]{:S(2)}, u32[]{:S(2)}) collective-permute-start(bf16[4,256,512]{2,1,0:T(8,128)(2,1)S(1)} %get-tuple-element.117), channel_id=1, source_target_pairs={{0,1},{1,0},{2,3},{3,2},{4,5},{5,4},{6,7},{7,6},{8,9},{9,8},{10,11... | collective-permute-start | bytes 3145736 | tf_op jit(solution)/shard_map/ppermute | solution.py:19
  99.4 15.4 %copy-start.3 = (s32[2]{0:T(128)S(1)}, s32[2]{0:T(128)}, u32[]{:S(2)}) copy-start(s32[2]{0:T(128)} %pad_add_fusion.1.scalars_ref) | copy-start | bytes 28
  103.7 10.5 %collective-permute-start.24 = (bf16[256,512]{1,0:T(8,128)(2,1)}, bf16[256,512]{1,0:T(8,128)(2,1)}, u32[]{:S(2)}, u32[]{:S(2)}) collective-permute-start(bf16[256,512]{1,0:T(8,128)(2,1)} %get-tuple-element.170), channel_id=1, source_target_pairs={{0,6},{1,7},{2,4},{3,5},{4,2},{5,3},{6,0},{7,1},{8,14},{9,15},{10,... | collective-permute-start | bytes 786440 | tf_op jit(solution)/shard_map/ppermute | solution.py:19
  105.3 39.8 %collective-permute-start.21 = (bf16[256,512]{1,0:T(8,128)(2,1)}, bf16[256,512]{1,0:T(8,128)(2,1)S(1)}, u32[]{:S(2)}, u32[]{:S(2)}) collective-permute-start(bf16[256,512]{1,0:T(8,128)(2,1)} %copy-done.14), channel_id=1, source_target_pairs={{0,6},{1,7},{2,4},{3,5},{4,2},{5,3},{6,0},{7,1},{8,14},{9,15},{10,... | collective-permute-start | bytes 786440 | tf_op jit(solution)/shard_map/ppermute | solution.py:19
  106.9 38.3 %collective-permute-start.20 = (bf16[256,512]{1,0:T(8,128)(2,1)}, bf16[256,512]{1,0:T(8,128)(2,1)S(1)}, u32[]{:S(2)}, u32[]{:S(2)}) collective-permute-start(bf16[256,512]{1,0:T(8,128)(2,1)} %copy-done.14), channel_id=1, source_target_pairs={{0,4},{1,5},{2,6},{3,7},{4,0},{5,1},{6,2},{7,3},{8,12},{9,13},{10,... | collective-permute-start | bytes 786440 | tf_op jit(solution)/shard_map/ppermute | solution.py:19
  107.8 37.4 %collective-permute-start.19 = (bf16[256,512]{1,0:T(8,128)(2,1)}, bf16[256,512]{1,0:T(8,128)(2,1)S(1)}, u32[]{:S(2)}, u32[]{:S(2)}) collective-permute-start(bf16[256,512]{1,0:T(8,128)(2,1)} %copy-done.14), channel_id=1, source_target_pairs={{0,2},{1,3},{2,0},{3,1},{4,6},{5,7},{6,4},{7,5},{8,10},{9,11},{10,... | collective-permute-start | bytes 786440 | tf_op jit(solution)/shard_map/ppermute | solution.py:19
  108.9 36.2 %collective-permute-start.23 = (bf16[256,512]{1,0:T(8,128)(2,1)}, bf16[256,512]{1,0:T(8,128)(2,1)S(1)}, u32[]{:S(2)}, u32[]{:S(2)}) collective-permute-start(bf16[256,512]{1,0:T(8,128)(2,1)} %get-tuple-element.171), channel_id=1, source_target_pairs={{0,4},{1,5},{2,6},{3,7},{4,0},{5,1},{6,2},{7,3},{8,12},{9,13},{10,... | collective-permute-start | bytes 786440 | tf_op jit(solution)/shard_map/ppermute | solution.py:19
  114.2 31.6 %copy-start.15 = (bf16[256,512]{1,0:T(8,128)(2,1)S(1)}, bf16[256,512]{1,0:T(8,128)(2,1)}, u32[]{:S(2)}) copy-start(bf16[256,512]{1,0:T(8,128)(2,1)} %copy-done.14) | copy-start | bytes 786436
  114.2 30.9 %collective-permute-start.22 = (bf16[256,512]{1,0:T(8,128)(2,1)}, bf16[256,512]{1,0:T(8,128)(2,1)S(1)}, u32[]{:S(2)}, u32[]{:S(2)}) collective-permute-start(bf16[256,512]{1,0:T(8,128)(2,1)} %get-tuple-element.172), channel_id=1, source_target_pairs={{0,2},{1,3},{2,0},{3,1},{4,6},{5,7},{6,4},{7,5},{8,10},{9,11},{10,... | collective-permute-start | bytes 786440 | tf_op jit(solution)/shard_map/ppermute | solution.py:19
  145.2 5.7 %collective-permute-start.25 = (bf16[4,512,512]{2,1,0:T(8,128)(2,1)S(1)}, bf16[4,512,512]{2,1,0:T(8,128)(2,1)S(1)}, u32[]{:S(2)}, u32[]{:S(2)}) collective-permute-start(bf16[4,512,512]{2,1,0:T(8,128)(2,1)S(1)} %get-tuple-element.140), channel_id=1, source_target_pairs={{0,1},{1,0},{2,3},{3,2},{4,5},{5,4},{6,7},{7,6},{8,9},{9,8},{10,11... | collective-permute-start | bytes 6291464 | tf_op jit(solution)/shard_map/ppermute | solution.py:19
  146.0 4.9 %collective-permute-start.26 = (bf16[4,256,512]{2,1,0:T(8,128)(2,1)S(1)}, bf16[4,256,512]{2,1,0:T(8,128)(2,1)S(1)}, u32[]{:S(2)}, u32[]{:S(2)}) collective-permute-start(bf16[4,256,512]{2,1,0:T(8,128)(2,1)S(1)} %pad_maximum_fusion.2.refs_0_), channel_id=1, source_target_pairs={{0,1},{1,0},{2,3},{3,2},{4,5},{5,4},{6,7},{7,6},{8,9},{9,8},{10,11... | collective-permute-start | bytes 3145736 | tf_op jit(solution)/shard_map/ppermute | solution.py:19
  151.5 21.2 %collective-permute-start.29 = (bf16[512,512]{1,0:T(8,128)(2,1)S(1)}, bf16[512,512]{1,0:T(8,128)(2,1)S(1)}, u32[]{:S(2)}, u32[]{:S(2)}) collective-permute-start(bf16[512,512]{1,0:T(8,128)(2,1)S(1)} %get-tuple-element.163), channel_id=1, source_target_pairs={{0,6},{1,7},{2,4},{3,5},{4,2},{5,3},{6,0},{7,1},{8,14},{9,15},{10,... | collective-permute-start | bytes 1572872 | tf_op jit(solution)/shard_map/ppermute | solution.py:19
  153.4 24.3 %collective-permute-start.28 = (bf16[512,512]{1,0:T(8,128)(2,1)S(1)}, bf16[512,512]{1,0:T(8,128)(2,1)S(1)}, u32[]{:S(2)}, u32[]{:S(2)}) collective-permute-start(bf16[512,512]{1,0:T(8,128)(2,1)S(1)} %get-tuple-element.164), channel_id=1, source_target_pairs={{0,4},{1,5},{2,6},{3,7},{4,0},{5,1},{6,2},{7,3},{8,12},{9,13},{10,... | collective-permute-start | bytes 1572872 | tf_op jit(solution)/shard_map/ppermute | solution.py:19
  154.5 23.2 %collective-permute-start.27 = (bf16[512,512]{1,0:T(8,128)(2,1)S(1)}, bf16[512,512]{1,0:T(8,128)(2,1)S(1)}, u32[]{:S(2)}, u32[]{:S(2)}) collective-permute-start(bf16[512,512]{1,0:T(8,128)(2,1)S(1)} %get-tuple-element.165), channel_id=1, source_target_pairs={{0,2},{1,3},{2,0},{3,1},{4,6},{5,7},{6,4},{7,5},{8,10},{9,11},{10,... | collective-permute-start | bytes 1572872 | tf_op jit(solution)/shard_map/ppermute | solution.py:19
  177.7 2.7 %collective-permute-start.32 = (bf16[4,256,512]{2,1,0:T(8,128)(2,1)S(1)}, bf16[4,256,512]{2,1,0:T(8,128)(2,1)S(1)}, u32[]{:S(2)}, u32[]{:S(2)}) collective-permute-start(bf16[4,256,512]{2,1,0:T(8,128)(2,1)S(1)} %get-tuple-element.160), channel_id=1, source_target_pairs={{0,1},{1,0},{2,3},{3,2},{4,5},{5,4},{6,7},{7,6},{8,9},{9,8},{10,11... | collective-permute-start | bytes 3145736 | tf_op jit(solution)/shard_map/ppermute | solution.py:19
  180.6 9.2 %collective-permute-start.33 = (bf16[256,512]{1,0:T(8,128)(2,1)S(1)}, bf16[256,512]{1,0:T(8,128)(2,1)S(1)}, u32[]{:S(2)}, u32[]{:S(2)}) collective-permute-start(bf16[256,512]{1,0:T(8,128)(2,1)S(1)} %get-tuple-element.167), channel_id=1, source_target_pairs={{0,2},{1,3},{2,0},{3,1},{4,6},{5,7},{6,4},{7,5},{8,10},{9,11},{10,... | collective-permute-start | bytes 786440 | tf_op jit(solution)/shard_map/ppermute | solution.py:19
  182.1 13.5 %collective-permute-start.35 = (bf16[256,512]{1,0:T(8,128)(2,1)S(1)}, bf16[256,512]{1,0:T(8,128)(2,1)S(1)}, u32[]{:S(2)}, u32[]{:S(2)}) collective-permute-start(bf16[256,512]{1,0:T(8,128)(2,1)S(1)} %get-tuple-element.168), channel_id=1, source_target_pairs={{0,6},{1,7},{2,4},{3,5},{4,2},{5,3},{6,0},{7,1},{8,14},{9,15},{10,... | collective-permute-start | bytes 786440 | tf_op jit(solution)/shard_map/ppermute | solution.py:19
  183.5 26.7 %copy-start.5 = (bf16[256,512]{1,0:T(8,128)(2,1)S(1)}, bf16[256,512]{1,0:T(8,128)(2,1)}, u32[]{:S(2)}) copy-start(bf16[256,512]{1,0:T(8,128)(2,1)} %copy-done.4) | copy-start | bytes 786436
  183.5 26.7 %copy-start.6 = (bf16[256,512]{1,0:T(8,128)(2,1)S(1)}, bf16[256,512]{1,0:T(8,128)(2,1)}, u32[]{:S(2)}) copy-start(bf16[256,512]{1,0:T(8,128)(2,1)} %get-tuple-element.133) | copy-start | bytes 786436
  183.5 26.7 %copy-start.9 = (bf16[256,512]{1,0:T(8,128)(2,1)S(1)}, bf16[256,512]{1,0:T(8,128)(2,1)}, u32[]{:S(2)}) copy-start(bf16[256,512]{1,0:T(8,128)(2,1)} %copy-done.8) | copy-start | bytes 786436
  183.5 13.4 %collective-permute-start.34 = (bf16[256,512]{1,0:T(8,128)(2,1)S(1)}, bf16[256,512]{1,0:T(8,128)(2,1)S(1)}, u32[]{:S(2)}, u32[]{:S(2)}) collective-permute-start(bf16[256,512]{1,0:T(8,128)(2,1)S(1)} %get-tuple-element.169), channel_id=1, source_target_pairs={{0,4},{1,5},{2,6},{3,7},{4,0},{5,1},{6,2},{7,3},{8,12},{9,13},{10,... | collective-permute-start | bytes 786440 | tf_op jit(solution)/shard_map/ppermute | solution.py:19
  184.5 13.1 %collective-permute-start.30 = (bf16[256,512]{1,0:T(8,128)(2,1)S(1)}, bf16[256,512]{1,0:T(8,128)(2,1)S(1)}, u32[]{:S(2)}, u32[]{:S(2)}) collective-permute-start(bf16[256,512]{1,0:T(8,128)(2,1)S(1)} %get-tuple-element.178), channel_id=1, source_target_pairs={{0,8},{8,0},{16,24},{24,16},{1,9},{9,1},{17,25},{25,17},{2,10},{10... | collective-permute-start | bytes 786440 | tf_op jit(solution)/shard_map/ppermute | solution.py:19
  186.1 11.6 %collective-permute-start.31 = (bf16[256,512]{1,0:T(8,128)(2,1)S(1)}, bf16[256,512]{1,0:T(8,128)(2,1)S(1)}, u32[]{:S(2)}, u32[]{:S(2)}) collective-permute-start(bf16[256,512]{1,0:T(8,128)(2,1)S(1)} %get-tuple-element.179), channel_id=1, source_target_pairs={{0,16},{8,24},{16,0},{24,8},{1,17},{9,25},{17,1},{25,9},{2,18},{10... | collective-permute-start | bytes 786440 | tf_op jit(solution)/shard_map/ppermute | solution.py:19
  197.1 13.1 %collective-permute-start.36 = (bf16[256,512]{1,0:T(8,128)(2,1)S(1)}, bf16[256,512]{1,0:T(8,128)(2,1)S(1)}, u32[]{:S(2)}, u32[]{:S(2)}) collective-permute-start(bf16[256,512]{1,0:T(8,128)(2,1)S(1)} %fusion.6), channel_id=1, source_target_pairs={{0,24},{8,16},{16,8},{24,0},{1,25},{9,17},{17,9},{25,1},{2,26},{10... | collective-permute-start | bytes 786440 | tf_op jit(solution)/shard_map/ppermute | solution.py:19
  (10 other events, 37.2 us)

commit v2 on v1

--- a/solution.py
+++ b/solution.py
@@ -20,29 +20,24 @@
 
 
 def attend_kernel(devices, groups, scaling, lengths_ref, rank_ref, *refs):
-    cached_ref, q_ref, kn_ref, vn_ref, ow_hbm, like_ref, other_ref, ow_ref, semaphore = refs
-    fetch = pltpu.make_async_copy(ow_hbm, ow_ref, semaphore)
-
-    @pl.when(pl.program_id(0) == 0)
-    def _():
-        fetch.start()
-
+    pieces, (q_ref, kn_ref, vn_ref, ow_ref, like_ref, other_ref) = refs[:devices], refs[devices:]
     rank = rank_ref[0]
     length = lengths_ref[pl.program_id(0)]
     key_heads, new_rows, width = kn_ref.shape
-    span = cached_ref.shape[4]
+    span = pieces[0].shape[3]
     columns = like_ref.shape[2]
     cached = devices * span
     column = lax.broadcasted_iota(jnp.int32, (new_rows, cached), 1)
-    far_bias = jnp.where(column < length, 0.0, masked_score)
+    place = (rank ^ (column // span)) * span + column % span
+    far_bias = jnp.where(place < length, 0.0, masked_score)
     row = lax.broadcasted_iota(jnp.int32, (new_rows, new_rows), 0)
     step = lax.broadcasted_iota(jnp.int32, (new_rows, new_rows), 1)
     near_bias = jnp.where(step <= row, 0.0, masked_score)
     bias = jnp.concatenate([far_bias, near_bias], axis=1)
     outs = []
     for head in range(key_heads):
-        keys = jnp.concatenate([cached_ref[d, head, 0, 0] for d in range(devices)] + [kn_ref[head]], axis=0)
-        values = jnp.concatenate([cached_ref[d, head, 1, 0] for d in range(devices)] + [vn_ref[head]], axis=0)
+        keys = jnp.concatenate([p[0, head, 0] for p in pieces] + [kn_ref[head]], axis=0)
+        values = jnp.concatenate([p[1, head, 0] for p in pieces] + [vn_ref[head]], axis=0)
         for g in range(groups):
             q = q_ref[head * groups + g]
             scores = (
@@ -56,11 +51,6 @@
             mixed = jnp.dot(weights.astype(bf16), values, preferred_element_type=f32)
             outs.append((mixed / total).astype(bf16))
     attention = jnp.concatenate(outs, axis=1)
-
-    @pl.when(pl.program_id(0) == 0)
-    def _():
-        fetch.wait()
-
     for target, parity in ((like_ref, 0), (other_ref, 1)):
         for i in range(devices // 2):
             first = pl.multiple_of((rank ^ (2 * i + parity)) * columns, columns)
@@ -69,14 +59,13 @@
 
 
 def attend(lengths, rank, cached, q, kn, vn, out_weight, scaling):
-    devices, key_heads, _, requests, span, width = cached.shape
+    devices = len(cached)
+    _, key_heads, requests, span, width = cached[0].shape
     heads, rows, _ = q.shape
     new_rows = rows // requests
     model = out_weight.shape[1]
     columns = model // devices
-    cached_spec = pl.BlockSpec(
-        (devices, key_heads, 2, 1, span, width), lambda r, *_: (0, 0, 0, r, 0, 0)
-    )
+    cached_spec = pl.BlockSpec((2, key_heads, 1, span, width), lambda r, *_: (0, 0, r, 0, 0))
     near_spec = pl.BlockSpec((key_heads, new_rows, width), lambda r, *_: (0, r, 0))
     out_spec = pl.BlockSpec((devices // 2, new_rows, columns), lambda r, *_: (0, r, 0))
     out_type = jax.ShapeDtypeStruct((devices // 2, rows, columns), bf16)
@@ -86,33 +75,62 @@
         grid_spec=pltpu.PrefetchScalarGridSpec(
             num_scalar_prefetch=2,
             grid=(requests,),
-            in_specs=[
-                cached_spec,
+            in_specs=[cached_spec] * devices
+            + [
                 pl.BlockSpec((heads, new_rows, width), lambda r, *_: (0, r, 0)),
                 near_spec,
                 near_spec,
-                pl.BlockSpec(memory_space=pl.ANY),
+                pl.BlockSpec(memory_space=pltpu.VMEM),
             ],
             out_specs=[out_spec, out_spec],
-            scratch_shapes=[pltpu.VMEM(out_weight.shape, bf16), pltpu.SemaphoreType.DMA],
         ),
         out_shape=[out_type, out_type],
-        compiler_params=pltpu.CompilerParams(vmem_limit_bytes=58 * MIB),
+        compiler_params=pltpu.CompilerParams(vmem_limit_bytes=24 * MIB),
         cost_estimate=pl.CostEstimate(
             flops=flops, bytes_accessed=8 * MIB, transcendentals=rows * heads * devices * span
         ),
         name="attend",
-    )(lengths, rank, cached, q, kn, vn, out_weight)
+    )(lengths, rank, *cached, q, kn, vn, out_weight)
+
+
+def hold_kernel(source_ref, target_ref, semaphores):
+    parts = semaphores.shape[0]
+    rows = source_ref.shape[0] // parts
+    copies = [
+        pltpu.make_async_copy(
+            source_ref.at[pl.ds(i * rows, rows)], target_ref.at[pl.ds(i * rows, rows)], semaphores.at[i]
+        )
+        for i in range(parts)
+    ]
+    for copy in copies:
+        copy.start()
+    for copy in copies:
+        copy.wait()
+
+
+def hold(weight):
+    return pl.pallas_call(
+        hold_kernel,
+        in_specs=[pl.BlockSpec(memory_space=pl.ANY)],
+        out_specs=pl.BlockSpec(memory_space=pltpu.VMEM),
+        out_shape=pltpu.VMEM(weight.shape, weight.dtype),
+        scratch_shapes=[pltpu.SemaphoreType.DMA((4,))],
+        compiler_params=pltpu.CompilerParams(vmem_limit_bytes=54 * MIB),
+        name="hold",
+    )(weight)
 
 
 def blocks_of(size, block):
     return [(first, min(block, size - first)) for first in range(0, size, block)]
 
 
-def units_kernel(devices, experts, scalars_ref, *refs):
+def units_kernel(devices, experts, whole, scalars_ref, *refs):
     like_ref, other_ref, gain_ref, router_ref, routes_ref = refs[:5]
-    gate_hbm, up_hbm, down_hbm, active_ref, weight_ref, odd_ref, down_ref = refs[5:12]
-    normed_ref, gate_ref, up_ref, down_odd_ref, semaphores = refs[12:]
+    gate_hbm, up_hbm, down_hbm, active_ref, weight_ref, odd_ref = refs[5:11]
+    if whole:
+        even_ref, normed_ref, gate_ref, up_ref, down_odd_ref, down_ref, semaphores = refs[11:]
+    else:
+        down_ref, normed_ref, gate_ref, up_ref, down_odd_ref, semaphores = refs[11:]
     spans = blocks_of(active_ref.shape[1], unit_block)
     count = len(spans)
 
@@ -185,21 +203,25 @@
         downs[i].wait()
         total = jnp.dot(active_ref[...], down_odd_ref[i], preferred_element_type=f32)
         odd_ref[i] = (total * weight_ref[:, 0:1]).astype(bf16)
-    for copy in downs[half:]:
-        copy.wait()
-
-
-def run_units(experts, scalars, like, other, gain, router, routes, weights):
+    for i in range(half):
+        downs[half + i].wait()
+        if whole:
+            total = jnp.dot(active_ref[...], down_ref[i], preferred_element_type=f32)
+            even_ref[i] = (total * weight_ref[:, 0:1]).astype(bf16)
+
+
+def run_units(experts, whole, scalars, like, other, gain, router, routes, weights):
     half, rows, columns = like.shape
     model, units = weights[0].shape
     in_vmem = pl.BlockSpec(memory_space=pltpu.VMEM)
     in_hbm = pl.BlockSpec(memory_space=pl.ANY)
     out_shape = [jax.ShapeDtypeStruct((rows, units), bf16), jax.ShapeDtypeStruct((rows, 128), f32)]
     out_shape.append(jax.ShapeDtypeStruct((half, rows, columns), bf16))
-    out_shape.append(pltpu.VMEM((half, units, columns), bf16))
+    down_half = pltpu.VMEM((half, units, columns), bf16)
+    out_shape.append(out_shape[-1] if whole else down_half)
     block = min(unit_block, units)
     return pl.pallas_call(
-        functools.partial(units_kernel, 2 * half, experts),
+        functools.partial(units_kernel, 2 * half, experts, whole),
         in_specs=[pl.BlockSpec(memory_space=pltpu.SMEM)] + [in_vmem] * 5 + [in_hbm] * len(weights),
         out_specs=[in_vmem] * len(out_shape),
         out_shape=out_shape,
@@ -207,10 +229,11 @@
             pltpu.VMEM((rows, model), bf16),
             pltpu.VMEM((2, model, block), bf16),
             pltpu.VMEM((2, model, block), bf16),
-            pltpu.VMEM((half, units, columns), bf16),
+            down_half,
+            *([down_half] if whole else []),
             pltpu.SemaphoreType.DMA((2 * len(blocks_of(units, block)) + 2 * half,)),
         ],
-        compiler_params=pltpu.CompilerParams(vmem_limit_bytes=38 * MIB),
+        compiler_params=pltpu.CompilerParams(vmem_limit_bytes=(48 if whole else 44) * MIB),
         cost_estimate=pl.CostEstimate(
             flops=4 * rows * model * units, bytes_accessed=6 * model * units, transcendentals=rows * units
         ),
@@ -245,19 +268,25 @@
     return lax.optimization_barrier(values)
 
 
-def between_chips(piece):
+def between_chips(piece, sums):
     devices = lax.axis_size("tp")
-    return [piece] + [xor_swap(piece, "tp", j) for j in range(2, devices, 2)]
+    near, spread = [piece], [None if sums is None else sums[0]]
+    for i in range(1, devices // 2):
+        if piece is None:
+            spread.append(xor_swap(sums[i], "tp", 2 * i))
+        elif sums is None:
+            near.append(xor_swap(piece, "tp", 2 * i))
+        else:
+            both = xor_swap(jnp.concatenate([piece, sums[i]], axis=0), "tp", 2 * i)
+            near.append(both[: piece.shape[0]])
+            spread.append(both[piece.shape[0] :])
+    return (None if piece is None else near), (None if sums is None else spread)
 
 
 def core_sums(like, arrived):
     return [
         (like[i].astype(f32) + arrived[i].astype(f32)).astype(bf16) for i in range(like.shape[0])
     ]
-
-
-def scatter_chips(sums):
-    return [sums[0]] + [xor_swap(x, "tp", 2 * i) for i, x in enumerate(sums) if i > 0]
 
 
 def add_up(parts):
@@ -294,11 +323,12 @@
     model = out_weight.shape[1]
     columns = model // devices
 
-    cache = jnp.stack([cache_keys, cache_values]).transpose(3, 0, 1, 2, 4)
-    if own_keys * devices != key_heads:
-        cache = jnp.repeat(cache, own_keys * devices // key_heads, axis=0)
-    cache = cache.reshape(devices, own_keys, *cache.shape[1:])
-    cached = lax.all_to_all(cache, "tp", split_axis=0, concat_axis=0, tiled=True)
+    cache = jnp.stack([cache_keys, cache_values]).transpose(0, 3, 1, 2, 4)
+
+    def slab(device):
+        return lax.dynamic_slice_in_dim(cache, device * heads // grouping, own_keys, 1)
+
+    cached = [slab(rank)] + [xor_swap(slab(rank ^ j), "tp", j) for j in range(1, devices)]
     first_key = rank * heads // grouping
     kn = lax.dynamic_slice_in_dim(key_new, first_key, own_keys, 1).transpose(1, 0, 2)
     vn = lax.dynamic_slice_in_dim(value_new, first_key, own_keys, 1).transpose(1, 0, 2)
@@ -311,14 +341,16 @@
     routing = jnp.pad(routing, ((0, 0), (0, -routing.shape[1] % 128)))
     gain = gain.reshape(devices, 1, columns)
     scalars = jnp.stack([rank, plane]).astype(jnp.int32)
-    cached, routing, gain, scalars, q, kn, vn = fence(cached, routing, gain, scalars, q, kn, vn)
+    cached, out_held, routing, gain, scalars, q, kn, vn = fence(
+        cached, hold(out_weight), routing, gain, scalars, q, kn, vn
+    )
 
     like, other = attend(
-        context_lengths, scalars[:1], cached, q, kn, vn, out_weight, width**-0.5
+        context_lengths, scalars[:1], cached, q, kn, vn, out_held, width**-0.5
     )
     sums = core_sums(like, xor_swap(other, "tp", 1))
     sums, own_routes = fence(sums, routes)
-    parts = scatter_chips(sums)
+    _, parts = between_chips(None, sums)
     chunk_routes = [own_routes] + [xor_swap(own_routes, "req", k) for k in range(1, planes)]
     parts, chunk_routes = fence(parts, chunk_routes)
     hidden = (residual.astype(f32) + add_up(parts)).astype(bf16)
@@ -335,37 +367,42 @@
         rows = jnp.stack(near)
         return rows, xor_swap(rows, "tp", 1)
 
-    near = between_chips(hidden)
+    near, _ = between_chips(hidden, None)
     pieces = {k: xor_swap(hidden, "req", k) for k in range(1, min(planes, 3))}
     near, pieces, own = fence(near, pieces, hidden)
     pieces |= {k: xor_swap(own, "req", k) for k in range(3, planes)}
     like, other = rows_of(near)
-    spread, back = {}, {}
-
-    def send_back():
-        for at in list(spread):
-            total = add_up(spread.pop(at))
-            for i, k in enumerate(groups[at]):
-                part = total[i * span : (i + 1) * span]
-                back[k] = xor_swap(part.astype(bf16), "req", k) if k else part
+    sums, back = None, {}
+
+    def send_back(at, parts):
+        total = add_up(parts)
+        for i, k in enumerate(groups[at]):
+            part = total[i * span : (i + 1) * span]
+            back[k] = xor_swap(part.astype(bf16), "req", k) if k else part
 
     for at, group in enumerate(groups):
         following = groups[at + 1] if at + 1 < len(groups) else None
-        near = between_chips(joined(pieces, following)) if following else []
+        near, spread = between_chips(joined(pieces, following) if following else None, sums)
         active, weight, odd, down = run_units(
-            planes, scalars, like, other, gain, routing, joined(chunk_routes, group), weights
+            planes, at == 0, scalars, like, other, gain, routing, joined(chunk_routes, group), weights
         )
-        near, spread, pieces, active, weight, odd, down = fence(
-            near, spread, pieces, active, weight, odd, down
-        )
+        active, weight, odd, down = fence(active, weight, odd, down)
         if following:
+            near, spread, pieces, active = fence(near, spread, pieces, active)
             like, other = rows_of(near)
-        send_back()
+            if spread:
+                send_back(at - 1, spread)
         arrived = xor_swap(odd, "tp", 1)
-        even = run_down(active, weight, down)
-        even, arrived, other, pieces = fence(even, arrived, other, pieces)
-        spread[at] = scatter_chips(core_sums(even, arrived))
-    send_back()
+        even = run_down(active, weight, down) if at > 0 else down
+        if following:
+            even, arrived, other, pieces = fence(even, arrived, other, pieces)
+        else:
+            even, arrived = fence(even, arrived)
+            if spread:
+                send_back(at - 1, spread)
+        sums = core_sums(even, arrived)
+    _, spread = between_chips(None, sums)
+    send_back(len(groups) - 1, spread)
     total = hidden.astype(f32)
     for k in range(planes):
         total += back[k].astype(f32)

time: 216 us -> 247 us (1.14)
  waiting for transfers between devices: 70.8 us -> 101 us
  Pallas kernels: 83 us -> 87.9 us
  local copies, waits for them, and re-layouts: 9.69 us -> 6.25 us
    ppermute x37 -> x41, waiting for transfers between devices: 60.3 us -> 101 us  [xor_swap(): return lax.ppermute(x, axis, [(i, i ^ mask) for i in range(size)])]
    all_to_all x1 -> x0, waiting for transfers between devices: 10.4 us -> none  [per_device(): lax.all_to_all(cache, 'tp', split_axis=0, concat_axis=0, tiled=True)]
    pallas_call x3 -> x4, Pallas kernels: 65.6 us -> 75.7 us  [the longest x3 73.5 us: run_units(): pl.pallas_call(functools.partial(units_kernel, 2 * half, experts, whole),...]
    ppermute x37 -> x41, starting transfers between devices: 35.5 us -> 41.8 us  [xor_swap(): return lax.ppermute(x, axis, [(i, i ^ mask) for i in range(size)])]
    all_to_all x1 -> x0, starting transfers between devices: 3.85 us -> none  [per_device(): lax.all_to_all(cache, 'tp', split_axis=0, concat_axis=0, tiled=True)]
    unnamed x44 -> x32, local copies, waits for them, and re-layouts: 4.69 us -> 1.14 us
    pallas_call x1, Pallas kernels: 9.22 us -> 6.11 us  [attend(): pl.pallas_call(functools.partial(attend_kernel, devices, heads // key_hea...]
    pallas_call x3 -> x2, Pallas kernels: 8.25 us -> 6 us  [run_down(): pl.pallas_call(down_kernel, in_specs=[in_vmem] * 3, out_specs=in_vmem, ou...]
  transfers between devices with their start and end apart: 38 -> 41, of which waited for: 18 -> 22; matrix products, arithmetic and copies ran while one was open for 4% -> 3% of each run, Pallas kernels for 35% -> 26%
where the time goes in v2:
time: 247 us; the launch traced here: 244 us
  waiting for transfers between devices  101 us (41%)
  Pallas kernels  87.9 us (36%)
  starting transfers between devices  41.8 us (17%)
  local copies, waits for them, and re-layouts  6.25 us (3%)
  other arithmetic  6.22 us (3%)
    ppermute x41, waiting for transfers between devices, xor_swap(): return lax.ppermute(x, axis, [(i, i ^ mask) for i in range(size)])  101 us
    pallas_call x3, Pallas kernels, run_units(): pl.pallas_call(functools.partial(units_kernel, 2 * half, experts, whole),...  73.5 us
    ppermute x41, starting transfers between devices, xor_swap(): return lax.ppermute(x, axis, [(i, i ^ mask) for i in range(size)])  41.8 us
    pallas_call x1, Pallas kernels, attend(): pl.pallas_call(functools.partial(attend_kernel, devices, heads // key_hea...  6.11 us
    pallas_call x2, Pallas kernels, run_down(): pl.pallas_call(down_kernel, in_specs=[in_vmem] * 3, out_specs=in_vmem, ou...  6 us
  transfers between devices with their start and end apart: 41, of which 22 were waited for; matrix products, arithmetic and copies ran while one was open for 3% of the time, Pallas kernels for 26%

profile of v2, /device:TPU:8, one launch (start us, length us, event | category | flops | bytes accessed | tf_op | source)
XLA Modules:
  0.0 243.6 jit_solution(3815352705476924983)
XLA Ops:
  0.0 1.4 copy_bitcast_fusion
  1.5 2.5 %collective-permute-start.5 = (bf16[2,1,2,128,128]{4,3,2,1,0:T(8,128)(2,1)S(1)}, bf16[2,1,2,128,128]{4,3,2,1,0:T(8,128)(2,1)S(1)}, u32[]{:S(2)}, u32[]{:S(2)}) collective-permute-start(bf16[2,1,2,128,128]{4,3,2,1,0:T(8,128)(2,1)S(1)} %get-tuple-element.172), channel_id=1, source_target_pairs={{0,6},{1,7},{2,4},{3,5},{4,2},{5,3},{6,0},{7,1},{8,14},{9,15},{10,... | collective-permute-start | bytes 393224 | tf_op jit(solution)/shard_map/ppermute | solution.py:19
  4.1 1.8 collective-permute-start.6
  5.9 1.5 collective-permute-start.1
  7.9 5.4 %collective-permute-done.4.refs_5_ = bf16[2,1,2,128,128]{4,3,2,1,0:T(8,128)(2,1)S(1)} collective-permute-done((bf16[2,1,2,128,128]{4,3,2,1,0:T(8,128)(2,1)S(1)}, bf16[2,1,2,128,128]{4,3,2,1,0:T(8,128)(2,1)S(1)}, u32[]{:S(2)}, u32[]{:S(2)}) %collective-permute-start.4) | collective-permute-done | bytes 131104 | tf_op jit(solution)/shard_map/ppermute | solution.py:19
  13.3 1.5 collective-permute-start.3
  14.9 1.5 constant_dynamic-slice_fusion
  16.9 2.2 hold.1.refs_11_
  19.1 1.2 pad.4.refs_3_
  20.4 6.1 %attend.1 = (bf16[4,256,512]{2,1,0:T(8,128)(2,1)S(1)}, bf16[4,256,512]{2,1,0:T(8,128)(2,1)S(1)}) custom-call(s32[2]{0:T(128)S(1)} %copy-done.1, s32[1]{0:T(128)S(1)} %bitcast.108, bf16[2,1,2,128,128]{4,3,2,1,0:T(8,128)(2,1)S(1)} %bitcast.105, bf16[2,1,2,128,128]{4,3,2,1,0:T(8,128)(2,1)S(1)} %collective-permute-done.refs_1_, ...), custom_call_target="tpu_custom_call" | custom-call | flops 1677721600 | bytes 8388608 | tf_op jit(solution)/shard_map/attend/pallas_call | solution.py:73
  26.6 2.6 %collective-permute-done.7 = bf16[4,256,512]{2,1,0:T(8,128)(2,1)S(1)} collective-permute-done((bf16[4,256,512]{2,1,0:T(8,128)(2,1)S(1)}, bf16[4,256,512]{2,1,0:T(8,128)(2,1)S(1)}, u32[]{:S(2)}, u32[]{:S(2)}) %collective-permute-start.7) | collective-permute-done | bytes 1048608 | tf_op jit(solution)/shard_map/ppermute | solution.py:19
  29.6 1.6 collective-permute-start.8
  31.7 1.5 collective-permute-start.10
  33.1 2.6 %collective-permute-start.12 = (s32[256,2]{0,1:T(2,128)S(1)}, s32[256,2]{0,1:T(2,128)S(1)}, u32[]{:S(2)}, u32[]{:S(2)}) collective-permute-start(s32[256,2]{0,1:T(2,128)S(1)} %copy-done.12), channel_id=1, source_target_pairs={{0,16},{8,24},{16,0},{24,8},{1,17},{9,25},{17,1},{25,9},{2,18},{10... | collective-permute-start | bytes 6152 | tf_op jit(solution)/shard_map/ppermute | solution.py:19
  36.3 1.3 collective-permute-done.12
  37.6 1.6 collective-permute-start.13
  39.3 4.7 %collective-permute-done.13.refs_4_ = s32[256,2]{1,0:T(8,128)S(1)} collective-permute-done((s32[256,2]{1,0:T(8,128)S(1)}, s32[256,2]{1,0:T(8,128)S(1)}, u32[]{:S(2)}, u32[]{:S(2)}) %collective-permute-start.13) | collective-permute-done | bytes 2080 | tf_op jit(solution)/shard_map/ppermute | solution.py:19
  45.0 2.7 %collective-permute-start.18 = (bf16[256,512]{1,0:T(8,128)(2,1)S(1)}, bf16[256,512]{1,0:T(8,128)(2,1)S(1)}, u32[]{:S(2)}, u32[]{:S(2)}) collective-permute-start(bf16[256,512]{1,0:T(8,128)(2,1)S(1)} %add_convert_fusion.13), channel_id=1, source_target_pairs={{0,16},{8,24},{16,0},{24,8},{1,17},{9,25},{17,1},{25,9},{2,18},{10... | collective-permute-start | bytes 786440 | tf_op jit(solution)/shard_map/ppermute | solution.py:19
  48.1 1.2 collective-permute-start.16
  50.2 1.4 collective-permute-start.14
  51.6 6.3 %collective-permute-done.18 = bf16[256,512]{1,0:T(8,128)(2,1)S(1)} collective-permute-done((bf16[256,512]{1,0:T(8,128)(2,1)S(1)}, bf16[256,512]{1,0:T(8,128)(2,1)S(1)}, u32[]{:S(2)}, u32[]{:S(2)}) %collective-permute-start.18) | collective-permute-done | bytes 262176 | tf_op jit(solution)/shard_map/ppermute | solution.py:19
  59.0 2.3 collective-permute-done.15
  61.3 1.6 collective-permute-start.23
  63.5 1.4 collective-permute-start.21
  65.6 13.8 %collective-permute-done.24 = bf16[256,512]{1,0:T(8,128)(2,1)S(1)} collective-permute-done((bf16[256,512]{1,0:T(8,128)(2,1)S(1)}, bf16[256,512]{1,0:T(8,128)(2,1)S(1)}, u32[]{:S(2)}, u32[]{:S(2)}) %collective-permute-start.24) | collective-permute-done | bytes 262176 | tf_op jit(solution)/shard_map/ppermute | solution.py:19
  79.4 7.9 %collective-permute-done.22 = bf16[512,512]{1,0:T(8,128)(2,1)S(1)} collective-permute-done((bf16[512,512]{1,0:T(8,128)(2,1)S(1)}, bf16[512,512]{1,0:T(8,128)(2,1)S(1)}, u32[]{:S(2)}, u32[]{:S(2)}) %collective-permute-start.22) | collective-permute-done | bytes 524320 | tf_op jit(solution)/shard_map/ppermute | solution.py:19
  87.4 1.6 pad_maximum_fusion.refs_0_
  89.1 21.9 %units.3 = (bf16[256,1792]{1,0:T(8,128)(2,1)}, f32[256,128]{1,0:T(8,128)}, bf16[4,256,512]{2,1,0:T(8,128)(2,1)}, bf16[4,256,512]{2,1,0:T(8,128)(2,1)S(1)}) custom-call(s32[2]{0:T(128)S(1)} %pad_add_fusion.1.scalars_ref, bf16[4,256,512]{2,1,0:T(8,128)(2,1)S(1)} %pad_maximum_fusion.1.refs_0_, bf16[4,256,512]{2,1,0:T(8,128)(2,1)S(1)} %collective-permute-done.19.refs_1_, ...), custom_call_target="tpu_custom_call" | custom-call | flops 7516192768 | bytes 44040192 | tf_op jit(solution)/shard_map/units/pallas_call | solution.py:223
  111.7 2.3 collective-permute-done.20
  115.6 1.6 collective-permute-start.28
  117.7 32.8 %units.4 = (bf16[512,1792]{1,0:T(8,128)(2,1)}, f32[512,128]{1,0:T(8,128)S(1)}, bf16[4,512,512]{2,1,0:T(8,128)(2,1)}, bf16[4,1792,512]{2,1,0:T(8,128)(2,1)S(1)}) custom-call(s32[2]{0:T(128)S(1)} %pad_add_fusion.1.scalars_ref, bf16[4,512,512]{2,1,0:T(8,128)(2,1)} %pad_maximum_fusion.refs_0_, bf16[4,512,512]{2,1,0:T(8,128)(2,1)} %collective-permute-done.25.refs_1_, ...), custom_call_target="tpu_custom_call" | custom-call | flops 15032385536 | bytes 44040192 | tf_op jit(solution)/shard_map/units/pallas_call | solution.py:223
  150.6 1.5 collective-permute-start.26
  152.2 12.8 %collective-permute-done.26 = bf16[512,512]{1,0:T(8,128)(2,1)S(1)} collective-permute-done((bf16[512,512]{1,0:T(8,128)(2,1)S(1)}, bf16[512,512]{1,0:T(8,128)(2,1)S(1)}, u32[]{:S(2)}, u32[]{:S(2)}) %collective-permute-start.26) | collective-permute-done | bytes 524320 | tf_op jit(solution)/shard_map/ppermute | solution.py:19
  165.2 3.9 %down.2 = bf16[4,512,512]{2,1,0:T(8,128)(2,1)S(1)} custom-call(bf16[512,1792]{1,0:T(8,128)(2,1)S(1)} %copy-done.2, f32[512,128]{1,0:T(8,128)S(1)} %get-tuple-element.135.weight_ref, bf16[4,1792,512]{2,1,0:T(8,128)(2,1)S(1)} %get-tuple-element.136.down_ref), custom_call_target="tpu_custom_call" | custom-call | flops 3758096384 | bytes 7340032 | tf_op jit(solution)/shard_map/down/pallas_call | solution.py:254
  170.2 18.9 %units.5 = (bf16[256,1792]{1,0:T(8,128)(2,1)S(1)}, f32[256,128]{1,0:T(8,128)S(1)}, bf16[4,256,512]{2,1,0:T(8,128)(2,1)S(1)}, bf16[4,1792,512]{2,1,0:T(8,128)(2,1)S(1)}) custom-call(s32[2]{0:T(128)S(1)} %pad_add_fusion.1.scalars_ref, bf16[4,256,512]{2,1,0:T(8,128)(2,1)} %copy-done.3, bf16[4,256,512]{2,1,0:T(8,128)(2,1)} %copy-done.6, ...), custom_call_target="tpu_custom_call" | custom-call | flops 7516192768 | bytes 44040192 | tf_op jit(solution)/shard_map/units/pallas_call | solution.py:223
  190.2 1.4 collective-permute-start.31
  191.6 1.5 collective-permute-start.33
  193.7 2.1 down.3
  196.0 1.4 collective-permute-start.37
  197.5 1.5 collective-permute-start.39
  199.0 6.0 %collective-permute-done.31 = bf16[512,512]{1,0:T(8,128)(2,1)S(1)} collective-permute-done((bf16[512,512]{1,0:T(8,128)(2,1)S(1)}, bf16[512,512]{1,0:T(8,128)(2,1)S(1)}, u32[]{:S(2)}, u32[]{:S(2)}) %collective-permute-start.31) | collective-permute-done | bytes 524320 | tf_op jit(solution)/shard_map/ppermute | solution.py:19
  205.0 1.4 collective-permute-start.38
  206.5 10.7 %collective-permute-done.33 = bf16[512,512]{1,0:T(8,128)(2,1)S(1)} collective-permute-done((bf16[512,512]{1,0:T(8,128)(2,1)S(1)}, bf16[512,512]{1,0:T(8,128)(2,1)S(1)}, u32[]{:S(2)}, u32[]{:S(2)}) %collective-permute-start.33) | collective-permute-done | bytes 524320 | tf_op jit(solution)/shard_map/ppermute | solution.py:19
  217.2 1.9 collective-permute-done.32
  219.5 1.6 collective-permute-start.34
  221.9 5.7 %collective-permute-done.39 = bf16[256,512]{1,0:T(8,128)(2,1)S(1)} collective-permute-done((bf16[256,512]{1,0:T(8,128)(2,1)S(1)}, bf16[256,512]{1,0:T(8,128)(2,1)S(1)}, u32[]{:S(2)}, u32[]{:S(2)}) %collective-permute-start.39) | collective-permute-done | bytes 262176 | tf_op jit(solution)/shard_map/ppermute | solution.py:19
  227.6 1.3 collective-permute-done.38
  229.8 12.5 %collective-permute-done.40 = bf16[256,512]{1,0:T(8,128)(2,1)S(1)} collective-permute-done((bf16[256,512]{1,0:T(8,128)(2,1)S(1)}, bf16[256,512]{1,0:T(8,128)(2,1)S(1)}, u32[]{:S(2)}, u32[]{:S(2)}) %collective-permute-start.40) | collective-permute-done | bytes 262176 | tf_op jit(solution)/shard_map/ppermute | solution.py:19
  (104 shorter events, 16.9 us)
Async XLA Ops:
  1.5 14.9 %copy-start.9 = (bf16[256,4,128]{2,1,0:T(4,128)(2,1)S(1)}, bf16[256,4,128]{2,1,0:T(4,128)(2,1)}, u32[]{:S(2)}) copy-start(bf16[256,4,128]{2,1,0:T(4,128)(2,1)} %param.14) | copy-start | bytes 786436
  1.5 6.3 %collective-permute-start.5 = (bf16[2,1,2,128,128]{4,3,2,1,0:T(8,128)(2,1)S(1)}, bf16[2,1,2,128,128]{4,3,2,1,0:T(8,128)(2,1)S(1)}, u32[]{:S(2)}, u32[]{:S(2)}) collective-permute-start(bf16[2,1,2,128,128]{4,3,2,1,0:T(8,128)(2,1)S(1)} %get-tuple-element.172), channel_id=1, source_target_pairs={{0,6},{1,7},{2,4},{3,5},{4,2},{5,3},{6,0},{7,1},{8,14},{9,15},{10,... | collective-permute-start | bytes 393224 | tf_op jit(solution)/shard_map/ppermute | solution.py:19
  4.0 9.3 %collective-permute-start.4 = (bf16[2,1,2,128,128]{4,3,2,1,0:T(8,128)(2,1)S(1)}, bf16[2,1,2,128,128]{4,3,2,1,0:T(8,128)(2,1)S(1)}, u32[]{:S(2)}, u32[]{:S(2)}) collective-permute-start(bf16[2,1,2,128,128]{4,3,2,1,0:T(8,128)(2,1)S(1)} %get-tuple-element.173), channel_id=1, source_target_pairs={{0,5},{1,4},{2,7},{3,6},{4,1},{5,0},{6,3},{7,2},{8,13},{9,12},{10,... | collective-permute-start | bytes 393224 | tf_op jit(solution)/shard_map/ppermute | solution.py:19
  4.1 16.3 %collective-permute-start.6 = (bf16[2,1,2,128,128]{4,3,2,1,0:T(8,128)(2,1)S(1)}, bf16[2,1,2,128,128]{4,3,2,1,0:T(8,128)(2,1)S(1)}, u32[]{:S(2)}, u32[]{:S(2)}) collective-permute-start(bf16[2,1,2,128,128]{4,3,2,1,0:T(8,128)(2,1)S(1)} %get-tuple-element.166), channel_id=1, source_target_pairs={{0,7},{1,6},{2,5},{3,4},{4,3},{5,2},{6,1},{7,0},{8,15},{9,14},{10,... | collective-permute-start | bytes 393224 | tf_op jit(solution)/shard_map/ppermute | solution.py:19
  5.9 14.5 %collective-permute-start = (bf16[2,1,2,128,128]{4,3,2,1,0:T(8,128)(2,1)S(1)}, bf16[2,1,2,128,128]{4,3,2,1,0:T(8,128)(2,1)S(1)}, u32[]{:S(2)}, u32[]{:S(2)}) collective-permute-start(bf16[2,1,2,128,128]{4,3,2,1,0:T(8,128)(2,1)S(1)} %get-tuple-element.168), channel_id=1, source_target_pairs={{0,1},{1,0},{2,3},{3,2},{4,5},{5,4},{6,7},{7,6},{8,9},{9,8},{10,11... | collective-permute-start | bytes 393224 | tf_op jit(solution)/shard_map/ppermute | solution.py:19
  5.9 14.5 %collective-permute-start.1 = (bf16[2,1,2,128,128]{4,3,2,1,0:T(8,128)(2,1)S(1)}, bf16[2,1,2,128,128]{4,3,2,1,0:T(8,128)(2,1)S(1)}, u32[]{:S(2)}, u32[]{:S(2)}) collective-permute-start(bf16[2,1,2,128,128]{4,3,2,1,0:T(8,128)(2,1)S(1)} %get-tuple-element.169), channel_id=1, source_target_pairs={{0,2},{1,3},{2,0},{3,1},{4,6},{5,7},{6,4},{7,5},{8,10},{9,11},{10,... | collective-permute-start | bytes 393224 | tf_op jit(solution)/shard_map/ppermute | solution.py:19
  7.8 12.5 %collective-permute-start.2 = (bf16[2,1,2,128,128]{4,3,2,1,0:T(8,128)(2,1)S(1)}, bf16[2,1,2,128,128]{4,3,2,1,0:T(8,128)(2,1)S(1)}, u32[]{:S(2)}, u32[]{:S(2)}) collective-permute-start(bf16[2,1,2,128,128]{4,3,2,1,0:T(8,128)(2,1)S(1)} %get-tuple-element.170), channel_id=1, source_target_pairs={{0,3},{1,2},{2,1},{3,0},{4,7},{5,6},{6,5},{7,4},{8,11},{9,10},{10,... | collective-permute-start | bytes 393224 | tf_op jit(solution)/shard_map/ppermute | solution.py:19
  13.3 7.1 %collective-permute-start.3 = (bf16[2,1,2,128,128]{4,3,2,1,0:T(8,128)(2,1)S(1)}, bf16[2,1,2,128,128]{4,3,2,1,0:T(8,128)(2,1)S(1)}, u32[]{:S(2)}, u32[]{:S(2)}) collective-permute-start(bf16[2,1,2,128,128]{4,3,2,1,0:T(8,128)(2,1)S(1)} %get-tuple-element.171), channel_id=1, source_target_pairs={{0,4},{1,5},{2,6},{3,7},{4,0},{5,1},{6,2},{7,3},{8,12},{9,13},{10,... | collective-permute-start | bytes 393224 | tf_op jit(solution)/shard_map/ppermute | solution.py:19
  26.5 18.3 %copy-start.10 = (bf16[256,512]{1,0:T(8,128)(2,1)S(1)}, bf16[256,512]{1,0:T(8,128)(2,1)}, u32[]{:S(2)}) copy-start(bf16[256,512]{1,0:T(8,128)(2,1)} %param.20) | copy-start | bytes 786436
  26.6 2.7 %collective-permute-start.7 = (bf16[4,256,512]{2,1,0:T(8,128)(2,1)S(1)}, bf16[4,256,512]{2,1,0:T(8,128)(2,1)S(1)}, u32[]{:S(2)}, u32[]{:S(2)}) collective-permute-start(bf16[4,256,512]{2,1,0:T(8,128)(2,1)S(1)} %get-tuple-element.94), channel_id=1, source_target_pairs={{0,1},{1,0},{2,3},{3,2},{4,5},{5,4},{6,7},{7,6},{8,9},{9,8},{10,11... | collective-permute-start | bytes 3145736 | tf_op jit(solution)/shard_map/ppermute | solution.py:19
  29.6 14.4 %collective-permute-start.8 = (bf16[256,512]{1,0:T(8,128)(2,1)S(1)}, bf16[256,512]{1,0:T(8,128)(2,1)S(1)}, u32[]{:S(2)}, u32[]{:S(2)}) collective-permute-start(bf16[256,512]{1,0:T(8,128)(2,1)S(1)} %get-tuple-element.96), channel_id=1, source_target_pairs={{0,2},{1,3},{2,0},{3,1},{4,6},{5,7},{6,4},{7,5},{8,10},{9,11},{10,... | collective-permute-start | bytes 786440 | tf_op jit(solution)/shard_map/ppermute | solution.py:19
  31.1 13.7 %collective-permute-start.9 = (bf16[256,512]{1,0:T(8,128)(2,1)S(1)}, bf16[256,512]{1,0:T(8,128)(2,1)S(1)}, u32[]{:S(2)}, u32[]{:S(2)}) collective-permute-start(bf16[256,512]{1,0:T(8,128)(2,1)S(1)} %get-tuple-element.97), channel_id=1, source_target_pairs={{0,4},{1,5},{2,6},{3,7},{4,0},{5,1},{6,2},{7,3},{8,12},{9,13},{10,... | collective-permute-start | bytes 786440 | tf_op jit(solution)/shard_map/ppermute | solution.py:19
  31.7 13.2 %collective-permute-start.10 = (bf16[256,512]{1,0:T(8,128)(2,1)S(1)}, bf16[256,512]{1,0:T(8,128)(2,1)S(1)}, u32[]{:S(2)}, u32[]{:S(2)}) collective-permute-start(bf16[256,512]{1,0:T(8,128)(2,1)S(1)} %get-tuple-element.98), channel_id=1, source_target_pairs={{0,6},{1,7},{2,4},{3,5},{4,2},{5,3},{6,0},{7,1},{8,14},{9,15},{10,... | collective-permute-start | bytes 786440 | tf_op jit(solution)/shard_map/ppermute | solution.py:19
  33.1 4.5 %collective-permute-start.12 = (s32[256,2]{0,1:T(2,128)S(1)}, s32[256,2]{0,1:T(2,128)S(1)}, u32[]{:S(2)}, u32[]{:S(2)}) collective-permute-start(s32[256,2]{0,1:T(2,128)S(1)} %copy-done.12), channel_id=1, source_target_pairs={{0,16},{8,24},{16,0},{24,8},{1,17},{9,25},{17,1},{25,9},{2,18},{10... | collective-permute-start | bytes 6152 | tf_op jit(solution)/shard_map/ppermute | solution.py:19
  35.7 3.6 %collective-permute-start.11 = (s32[256,2]{0,1:T(2,128)S(1)}, s32[256,2]{0,1:T(2,128)S(1)}, u32[]{:S(2)}, u32[]{:S(2)}) collective-permute-start(s32[256,2]{0,1:T(2,128)S(1)} %copy-done.12), channel_id=1, source_target_pairs={{0,8},{8,0},{16,24},{24,16},{1,9},{9,1},{17,25},{25,17},{2,10},{10... | collective-permute-start | bytes 6152 | tf_op jit(solution)/shard_map/ppermute | solution.py:19
  37.6 6.4 %collective-permute-start.13 = (s32[256,2]{1,0:T(8,128)S(1)}, s32[256,2]{1,0:T(8,128)S(1)}, u32[]{:S(2)}, u32[]{:S(2)}) collective-permute-start(s32[256,2]{1,0:T(8,128)S(1)} %copy.57), channel_id=1, source_target_pairs={{0,24},{8,16},{16,8},{24,0},{1,25},{9,17},{17,9},{25,1},{2,26},{10... | collective-permute-start | bytes 6152 | tf_op jit(solution)/shard_map/ppermute | solution.py:19
  45.0 44.0 %copy-start.4 = (bf16[256,512]{1,0:T(8,128)(2,1)}, bf16[256,512]{1,0:T(8,128)(2,1)S(1)}, u32[]{:S(2)}) copy-start(bf16[256,512]{1,0:T(8,128)(2,1)S(1)} %add_convert_fusion.13) | copy-start | bytes 786436
  45.0 12.9 %collective-permute-start.18 = (bf16[256,512]{1,0:T(8,128)(2,1)S(1)}, bf16[256,512]{1,0:T(8,128)(2,1)S(1)}, u32[]{:S(2)}, u32[]{:S(2)}) collective-permute-start(bf16[256,512]{1,0:T(8,128)(2,1)S(1)} %add_convert_fusion.13), channel_id=1, source_target_pairs={{0,16},{8,24},{16,0},{24,8},{1,17},{9,25},{17,1},{25,9},{2,18},{10... | collective-permute-start | bytes 786440 | tf_op jit(solution)/shard_map/ppermute | solution.py:19
  47.7 11.3 %collective-permute-start.17 = (bf16[256,512]{1,0:T(8,128)(2,1)S(1)}, bf16[256,512]{1,0:T(8,128)(2,1)S(1)}, u32[]{:S(2)}, u32[]{:S(2)}) collective-permute-start(bf16[256,512]{1,0:T(8,128)(2,1)S(1)} %add_convert_fusion.13), channel_id=1, source_target_pairs={{0,8},{8,0},{16,24},{24,16},{1,9},{9,1},{17,25},{25,17},{2,10},{10... | collective-permute-start | bytes 786440 | tf_op jit(solution)/shard_map/ppermute | solution.py:19
  48.1 10.8 %collective-permute-start.16 = (bf16[256,512]{1,0:T(8,128)(2,1)S(1)}, bf16[256,512]{1,0:T(8,128)(2,1)S(1)}, u32[]{:S(2)}, u32[]{:S(2)}) collective-permute-start(bf16[256,512]{1,0:T(8,128)(2,1)S(1)} %add_convert_fusion.13), channel_id=1, source_target_pairs={{0,6},{1,7},{2,4},{3,5},{4,2},{5,3},{6,0},{7,1},{8,14},{9,15},{10,... | collective-permute-start | bytes 786440 | tf_op jit(solution)/shard_map/ppermute | solution.py:19
  49.3 12.0 %collective-permute-start.15 = (bf16[256,512]{1,0:T(8,128)(2,1)S(1)}, bf16[256,512]{1,0:T(8,128)(2,1)S(1)}, u32[]{:S(2)}, u32[]{:S(2)}) collective-permute-start(bf16[256,512]{1,0:T(8,128)(2,1)S(1)} %add_convert_fusion.13), channel_id=1, source_target_pairs={{0,4},{1,5},{2,6},{3,7},{4,0},{5,1},{6,2},{7,3},{8,12},{9,13},{10,... | collective-permute-start | bytes 786440 | tf_op jit(solution)/shard_map/ppermute | solution.py:19
  50.2 11.1 %collective-permute-start.14 = (bf16[256,512]{1,0:T(8,128)(2,1)S(1)}, bf16[256,512]{1,0:T(8,128)(2,1)S(1)}, u32[]{:S(2)}, u32[]{:S(2)}) collective-permute-start(bf16[256,512]{1,0:T(8,128)(2,1)S(1)} %add_convert_fusion.13), channel_id=1, source_target_pairs={{0,2},{1,3},{2,0},{3,1},{4,6},{5,7},{6,4},{7,5},{8,10},{9,11},{10,... | collective-permute-start | bytes 786440 | tf_op jit(solution)/shard_map/ppermute | solution.py:19
  61.3 18.1 %collective-permute-start.23 = (bf16[512,512]{1,0:T(8,128)(2,1)S(1)}, bf16[512,512]{1,0:T(8,128)(2,1)S(1)}, u32[]{:S(2)}, u32[]{:S(2)}) collective-permute-start(bf16[512,512]{1,0:T(8,128)(2,1)S(1)} %constant_dynamic-update-slice_fusion), channel_id=1, source_target_pairs={{0,6},{1,7},{2,4},{3,5},{4,2},{5,3},{6,0},{7,1},{8,14},{9,15},{10,... | collective-permute-start | bytes 1572872 | tf_op jit(solution)/shard_map/ppermute | solution.py:19
  62.9 24.5 %collective-permute-start.22 = (bf16[512,512]{1,0:T(8,128)(2,1)S(1)}, bf16[512,512]{1,0:T(8,128)(2,1)S(1)}, u32[]{:S(2)}, u32[]{:S(2)}) collective-permute-start(bf16[512,512]{1,0:T(8,128)(2,1)S(1)} %constant_dynamic-update-slice_fusion), channel_id=1, source_target_pairs={{0,4},{1,5},{2,6},{3,7},{4,0},{5,1},{6,2},{7,3},{8,12},{9,13},{10,... | collective-permute-start | bytes 1572872 | tf_op jit(solution)/shard_map/ppermute | solution.py:19
  63.5 23.9 %collective-permute-start.21 = (bf16[512,512]{1,0:T(8,128)(2,1)S(1)}, bf16[512,512]{1,0:T(8,128)(2,1)S(1)}, u32[]{:S(2)}, u32[]{:S(2)}) collective-permute-start(bf16[512,512]{1,0:T(8,128)(2,1)S(1)} %constant_dynamic-update-slice_fusion), channel_id=1, source_target_pairs={{0,2},{1,3},{2,0},{3,1},{4,6},{5,7},{6,4},{7,5},{8,10},{9,11},{10,... | collective-permute-start | bytes 1572872 | tf_op jit(solution)/shard_map/ppermute | solution.py:19
  65.0 24.1 %collective-permute-start.19 = (bf16[4,256,512]{2,1,0:T(8,128)(2,1)S(1)}, bf16[4,256,512]{2,1,0:T(8,128)(2,1)S(1)}, u32[]{:S(2)}, u32[]{:S(2)}) collective-permute-start(bf16[4,256,512]{2,1,0:T(8,128)(2,1)S(1)} %pad_maximum_fusion.1.refs_0_), channel_id=1, source_target_pairs={{0,1},{1,0},{2,3},{3,2},{4,5},{5,4},{6,7},{7,6},{8,9},{9,8},{10,11... | collective-permute-start | bytes 3145736 | tf_op jit(solution)/shard_map/ppermute | solution.py:19
  65.1 14.3 %collective-permute-start.24 = (bf16[256,512]{1,0:T(8,128)(2,1)S(1)}, bf16[256,512]{1,0:T(8,128)(2,1)S(1)}, u32[]{:S(2)}, u32[]{:S(2)}) collective-permute-start(bf16[256,512]{1,0:T(8,128)(2,1)S(1)} %add_convert_fusion.13), channel_id=1, source_target_pairs={{0,24},{8,16},{16,8},{24,0},{1,25},{9,17},{17,9},{25,1},{2,26},{10... | collective-permute-start | bytes 786440 | tf_op jit(solution)/shard_map/ppermute | solution.py:19
  79.4 7.9 %copy-start.7 = (bf16[256,512]{1,0:T(8,128)(2,1)}, bf16[256,512]{1,0:T(8,128)(2,1)S(1)}, u32[]{:S(2)}) copy-start(bf16[256,512]{1,0:T(8,128)(2,1)S(1)} %collective-permute-done.24) | copy-start | bytes 786436
  89.0 25.1 %collective-permute-start.25 = (bf16[4,512,512]{2,1,0:T(8,128)(2,1)}, bf16[4,512,512]{2,1,0:T(8,128)(2,1)}, u32[]{:S(2)}, u32[]{:S(2)}) collective-permute-start(bf16[4,512,512]{2,1,0:T(8,128)(2,1)} %pad_maximum_fusion.refs_0_), channel_id=1, source_target_pairs={{0,1},{1,0},{2,3},{3,2},{4,5},{5,4},{6,7},{7,6},{8,9},{9,8},{10,11... | collective-permute-start | bytes 6291464 | tf_op jit(solution)/shard_map/ppermute | solution.py:19
  111.0 3.1 %collective-permute-start.20 = (bf16[4,256,512]{2,1,0:T(8,128)(2,1)}, bf16[4,256,512]{2,1,0:T(8,128)(2,1)S(1)}, u32[]{:S(2)}, u32[]{:S(2)}) collective-permute-start(bf16[4,256,512]{2,1,0:T(8,128)(2,1)} %get-tuple-element.114), channel_id=1, source_target_pairs={{0,1},{1,0},{2,3},{3,2},{4,5},{5,4},{6,7},{7,6},{8,9},{9,8},{10,11... | collective-permute-start | bytes 3145736 | tf_op jit(solution)/shard_map/ppermute | solution.py:19
  115.6 36.5 %collective-permute-start.28 = (bf16[512,512]{1,0:T(8,128)(2,1)S(1)}, bf16[512,512]{1,0:T(8,128)(2,1)S(1)}, u32[]{:S(2)}, u32[]{:S(2)}) collective-permute-start(bf16[512,512]{1,0:T(8,128)(2,1)S(1)} %get-tuple-element.182), channel_id=1, source_target_pairs={{0,6},{1,7},{2,4},{3,5},{4,2},{5,3},{6,0},{7,1},{8,14},{9,15},{10,... | collective-permute-start | bytes 1572872 | tf_op jit(solution)/shard_map/ppermute | solution.py:19
  117.1 35.0 %collective-permute-start.27 = (bf16[512,512]{1,0:T(8,128)(2,1)S(1)}, bf16[512,512]{1,0:T(8,128)(2,1)S(1)}, u32[]{:S(2)}, u32[]{:S(2)}) collective-permute-start(bf16[512,512]{1,0:T(8,128)(2,1)S(1)} %get-tuple-element.183), channel_id=1, source_target_pairs={{0,4},{1,5},{2,6},{3,7},{4,0},{5,1},{6,2},{7,3},{8,12},{9,13},{10,... | collective-permute-start | bytes 1572872 | tf_op jit(solution)/shard_map/ppermute | solution.py:19
  150.5 14.5 %copy-start.8 = (bf16[256,512]{1,0:T(8,128)(2,1)S(1)}, bf16[256,512]{1,0:T(8,128)(2,1)}, u32[]{:S(2)}) copy-start(bf16[256,512]{1,0:T(8,128)(2,1)} %copy-done.7) | copy-start | bytes 786436
  150.5 18.7 %collective-permute-start.29 = (bf16[4,512,512]{2,1,0:T(8,128)(2,1)}, bf16[4,512,512]{2,1,0:T(8,128)(2,1)S(1)}, u32[]{:S(2)}, u32[]{:S(2)}) collective-permute-start(bf16[4,512,512]{2,1,0:T(8,128)(2,1)} %get-tuple-element.137), channel_id=1, source_target_pairs={{0,1},{1,0},{2,3},{3,2},{4,5},{5,4},{6,7},{7,6},{8,9},{9,8},{10,11... | collective-permute-start | bytes 6291464 | tf_op jit(solution)/shard_map/ppermute | solution.py:19
  150.6 14.3 %collective-permute-start.26 = (bf16[512,512]{1,0:T(8,128)(2,1)S(1)}, bf16[512,512]{1,0:T(8,128)(2,1)S(1)}, u32[]{:S(2)}, u32[]{:S(2)}) collective-permute-start(bf16[512,512]{1,0:T(8,128)(2,1)S(1)} %get-tuple-element.184), channel_id=1, source_target_pairs={{0,2},{1,3},{2,0},{3,1},{4,6},{5,7},{6,4},{7,5},{8,10},{9,11},{10,... | collective-permute-start | bytes 1572872 | tf_op jit(solution)/shard_map/ppermute | solution.py:19
  152.1 13.1 %copy-start.2 = (bf16[512,1792]{1,0:T(8,128)(2,1)S(1)}, bf16[512,1792]{1,0:T(8,128)(2,1)}, u32[]{:S(2)}) copy-start(bf16[512,1792]{1,0:T(8,128)(2,1)} %get-tuple-element.134.active_ref) | copy-start | bytes 5505028
  165.1 4.1 %collective-permute-start.30 = (bf16[4,256,512]{2,1,0:T(8,128)(2,1)S(1)}, bf16[4,256,512]{2,1,0:T(8,128)(2,1)S(1)}, u32[]{:S(2)}, u32[]{:S(2)}) collective-permute-start(bf16[4,256,512]{2,1,0:T(8,128)(2,1)S(1)} %pad_maximum_fusion.2.refs_0_), channel_id=1, source_target_pairs={{0,1},{1,0},{2,3},{3,2},{4,5},{5,4},{6,7},{7,6},{8,9},{9,8},{10,11... | collective-permute-start | bytes 3145736 | tf_op jit(solution)/shard_map/ppermute | solution.py:19
  189.1 6.6 %collective-permute-start.36 = (bf16[4,256,512]{2,1,0:T(8,128)(2,1)S(1)}, bf16[4,256,512]{2,1,0:T(8,128)(2,1)S(1)}, u32[]{:S(2)}, u32[]{:S(2)}) collective-permute-start(bf16[4,256,512]{2,1,0:T(8,128)(2,1)S(1)} %get-tuple-element.149), channel_id=1, source_target_pairs={{0,1},{1,0},{2,3},{3,2},{4,5},{5,4},{6,7},{7,6},{8,9},{9,8},{10,11... | collective-permute-start | bytes 3145736 | tf_op jit(solution)/shard_map/ppermute | solution.py:19
  190.2 14.9 %collective-permute-start.31 = (bf16[512,512]{1,0:T(8,128)(2,1)S(1)}, bf16[512,512]{1,0:T(8,128)(2,1)S(1)}, u32[]{:S(2)}, u32[]{:S(2)}) collective-permute-start(bf16[512,512]{1,0:T(8,128)(2,1)S(1)} %get-tuple-element.152), channel_id=1, source_target_pairs={{0,2},{1,3},{2,0},{3,1},{4,6},{5,7},{6,4},{7,5},{8,10},{9,11},{10,... | collective-permute-start | bytes 1572872 | tf_op jit(solution)/shard_map/ppermute | solution.py:19
  191.6 25.6 %collective-permute-start.33 = (bf16[512,512]{1,0:T(8,128)(2,1)S(1)}, bf16[512,512]{1,0:T(8,128)(2,1)S(1)}, u32[]{:S(2)}, u32[]{:S(2)}) collective-permute-start(bf16[512,512]{1,0:T(8,128)(2,1)S(1)} %get-tuple-element.153), channel_id=1, source_target_pairs={{0,6},{1,7},{2,4},{3,5},{4,2},{5,3},{6,0},{7,1},{8,14},{9,15},{10,... | collective-permute-start | bytes 1572872 | tf_op jit(solution)/shard_map/ppermute | solution.py:19
  193.1 25.9 %collective-permute-start.32 = (bf16[512,512]{1,0:T(8,128)(2,1)S(1)}, bf16[512,512]{1,0:T(8,128)(2,1)S(1)}, u32[]{:S(2)}, u32[]{:S(2)}) collective-permute-start(bf16[512,512]{1,0:T(8,128)(2,1)S(1)} %get-tuple-element.154), channel_id=1, source_target_pairs={{0,4},{1,5},{2,6},{3,7},{4,0},{5,1},{6,2},{7,3},{8,12},{9,13},{10,... | collective-permute-start | bytes 1572872 | tf_op jit(solution)/shard_map/ppermute | solution.py:19
  196.0 25.9 %collective-permute-start.37 = (bf16[256,512]{1,0:T(8,128)(2,1)S(1)}, bf16[256,512]{1,0:T(8,128)(2,1)S(1)}, u32[]{:S(2)}, u32[]{:S(2)}) collective-permute-start(bf16[256,512]{1,0:T(8,128)(2,1)S(1)} %get-tuple-element.155), channel_id=1, source_target_pairs={{0,2},{1,3},{2,0},{3,1},{4,6},{5,7},{6,4},{7,5},{8,10},{9,11},{10,... | collective-permute-start | bytes 786440 | tf_op jit(solution)/shard_map/ppermute | solution.py:19
  197.5 30.1 %collective-permute-start.39 = (bf16[256,512]{1,0:T(8,128)(2,1)S(1)}, bf16[256,512]{1,0:T(8,128)(2,1)S(1)}, u32[]{:S(2)}, u32[]{:S(2)}) collective-permute-start(bf16[256,512]{1,0:T(8,128)(2,1)S(1)} %get-tuple-element.156), channel_id=1, source_target_pairs={{0,6},{1,7},{2,4},{3,5},{4,2},{5,3},{6,0},{7,1},{8,14},{9,15},{10,... | collective-permute-start | bytes 786440 | tf_op jit(solution)/shard_map/ppermute | solution.py:19
  205.0 23.9 %collective-permute-start.38 = (bf16[256,512]{1,0:T(8,128)(2,1)S(1)}, bf16[256,512]{1,0:T(8,128)(2,1)S(1)}, u32[]{:S(2)}, u32[]{:S(2)}) collective-permute-start(bf16[256,512]{1,0:T(8,128)(2,1)S(1)} %get-tuple-element.157), channel_id=1, source_target_pairs={{0,4},{1,5},{2,6},{3,7},{4,0},{5,1},{6,2},{7,3},{8,12},{9,13},{10,... | collective-permute-start | bytes 786440 | tf_op jit(solution)/shard_map/ppermute | solution.py:19
  219.4 22.8 %copy-start.5 = (bf16[256,512]{1,0:T(8,128)(2,1)S(1)}, bf16[256,512]{1,0:T(8,128)(2,1)}, u32[]{:S(2)}) copy-start(bf16[256,512]{1,0:T(8,128)(2,1)} %copy-done.4) | copy-start | bytes 786436
  219.5 10.1 %collective-permute-start.34 = (bf16[256,512]{1,0:T(8,128)(2,1)S(1)}, bf16[256,512]{1,0:T(8,128)(2,1)S(1)}, u32[]{:S(2)}, u32[]{:S(2)}) collective-permute-start(bf16[256,512]{1,0:T(8,128)(2,1)S(1)} %get-tuple-element.174), channel_id=1, source_target_pairs={{0,8},{8,0},{16,24},{24,16},{1,9},{9,1},{17,25},{25,17},{2,10},{10... | collective-permute-start | bytes 786440 | tf_op jit(solution)/shard_map/ppermute | solution.py:19
  221.1 8.6 %collective-permute-start.35 = (bf16[256,512]{1,0:T(8,128)(2,1)S(1)}, bf16[256,512]{1,0:T(8,128)(2,1)S(1)}, u32[]{:S(2)}, u32[]{:S(2)}) collective-permute-start(bf16[256,512]{1,0:T(8,128)(2,1)S(1)} %get-tuple-element.175), channel_id=1, source_target_pairs={{0,16},{8,24},{16,0},{24,8},{1,17},{9,25},{17,1},{25,9},{2,18},{10... | collective-permute-start | bytes 786440 | tf_op jit(solution)/shard_map/ppermute | solution.py:19
  229.1 13.1 %collective-permute-start.40 = (bf16[256,512]{1,0:T(8,128)(2,1)S(1)}, bf16[256,512]{1,0:T(8,128)(2,1)S(1)}, u32[]{:S(2)}, u32[]{:S(2)}) collective-permute-start(bf16[256,512]{1,0:T(8,128)(2,1)S(1)} %fusion.9), channel_id=1, source_target_pairs={{0,24},{8,16},{16,8},{24,0},{1,25},{9,17},{17,9},{25,1},{2,26},{10... | collective-permute-start | bytes 786440 | tf_op jit(solution)/shard_map/ppermute | solution.py:19
  (7 other events, 28.2 us)

commit v3 on v2

--- a/solution.py
+++ b/solution.py
@@ -386,20 +386,16 @@
         active, weight, odd, down = run_units(
             planes, at == 0, scalars, like, other, gain, routing, joined(chunk_routes, group), weights
         )
-        active, weight, odd, down = fence(active, weight, odd, down)
+        near, spread, pieces, active, weight, odd, down = fence(
+            near, spread, pieces, active, weight, odd, down
+        )
         if following:
-            near, spread, pieces, active = fence(near, spread, pieces, active)
             like, other = rows_of(near)
-            if spread:
-                send_back(at - 1, spread)
+        if spread:
+            send_back(at - 1, spread)
         arrived = xor_swap(odd, "tp", 1)
         even = run_down(active, weight, down) if at > 0 else down
-        if following:
-            even, arrived, other, pieces = fence(even, arrived, other, pieces)
-        else:
-            even, arrived = fence(even, arrived)
-            if spread:
-                send_back(at - 1, spread)
+        even, arrived, other, pieces = fence(even, arrived, other, pieces)
         sums = core_sums(even, arrived)
     _, spread = between_chips(None, sums)
     send_back(len(groups) - 1, spread)

time: 247 us -> 207 us (0.84)
  waiting for transfers between devices: 101 us -> 58.6 us
    ppermute x41, waiting for transfers between devices: 101 us -> 58.6 us  [xor_swap(): return lax.ppermute(x, axis, [(i, i ^ mask) for i in range(size)])]
  transfers between devices with their start and end apart: 41 -> 41, of which waited for: 22 -> 21; matrix products, arithmetic and copies ran while one was open for 3% -> 2% of each run, Pallas kernels for 26% -> 40%
where the time goes in v3:
time: 207 us; the launch traced here: 204 us
  Pallas kernels  87.6 us (42%)
  waiting for transfers between devices  58.6 us (28%)
  starting transfers between devices  41.5 us (20%)
  other arithmetic  7.94 us (4%)
  local copies, waits for them, and re-layouts  7.08 us (3%)
    pallas_call x3, Pallas kernels, run_units(): pl.pallas_call(functools.partial(units_kernel, 2 * half, experts, whole),...  73.3 us
    ppermute x41, waiting for transfers between devices, xor_swap(): return lax.ppermute(x, axis, [(i, i ^ mask) for i in range(size)])  58.6 us
    ppermute x41, starting transfers between devices, xor_swap(): return lax.ppermute(x, axis, [(i, i ^ mask) for i in range(size)])  41.5 us
    pallas_call x1, Pallas kernels, attend(): pl.pallas_call(functools.partial(attend_kernel, devices, heads // key_hea...  6.1 us
    pallas_call x2, Pallas kernels, run_down(): pl.pallas_call(down_kernel, in_specs=[in_vmem] * 3, out_specs=in_vmem, ou...  6 us
  transfers between devices with their start and end apart: 41, of which 21 were waited for; matrix products, arithmetic and copies ran while one was open for 2% of the time, Pallas kernels for 40%

profile of v3, /device:TPU:8, one launch (start us, length us, event | category | flops | bytes accessed | tf_op | source)
XLA Modules:
  0.0 203.7 jit_solution(17998639267339474493)
XLA Ops:
  0.0 1.4 copy_bitcast_fusion
  1.5 2.5 %collective-permute-start.5 = (bf16[2,1,2,128,128]{4,3,2,1,0:T(8,128)(2,1)S(1)}, bf16[2,1,2,128,128]{4,3,2,1,0:T(8,128)(2,1)S(1)}, u32[]{:S(2)}, u32[]{:S(2)}) collective-permute-start(bf16[2,1,2,128,128]{4,3,2,1,0:T(8,128)(2,1)S(1)} %get-tuple-element.192), channel_id=1, source_target_pairs={{0,6},{1,7},{2,4},{3,5},{4,2},{5,3},{6,0},{7,1},{8,14},{9,15},{10,... | collective-permute-start | bytes 393224 | tf_op jit(solution)/shard_map/ppermute | solution.py:19
  4.1 1.8 collective-permute-start.6
  5.9 1.5 collective-permute-start.1
  7.9 5.4 %collective-permute-done.4.refs_5_ = bf16[2,1,2,128,128]{4,3,2,1,0:T(8,128)(2,1)S(1)} collective-permute-done((bf16[2,1,2,128,128]{4,3,2,1,0:T(8,128)(2,1)S(1)}, bf16[2,1,2,128,128]{4,3,2,1,0:T(8,128)(2,1)S(1)}, u32[]{:S(2)}, u32[]{:S(2)}) %collective-permute-start.4) | collective-permute-done | bytes 131104 | tf_op jit(solution)/shard_map/ppermute | solution.py:19
  13.3 1.5 collective-permute-start.3
  14.9 1.5 constant_dynamic-slice_fusion
  16.9 2.2 %hold.1.refs_11_ = bf16[512,4096]{1,0:T(8,128)(2,1)S(1)} custom-call(bf16[512,4096]{1,0:T(8,128)(2,1)} %source_ref.1), custom_call_target="tpu_custom_call" | custom-call | tf_op jit(solution)/shard_map/hold/pallas_call | solution.py:112
  19.1 1.2 pad.4.refs_3_
  20.4 6.1 %attend.1 = (bf16[4,256,512]{2,1,0:T(8,128)(2,1)S(1)}, bf16[4,256,512]{2,1,0:T(8,128)(2,1)S(1)}) custom-call(s32[2]{0:T(128)S(1)} %copy-done.1, s32[1]{0:T(128)S(1)} %bitcast.105, bf16[2,1,2,128,128]{4,3,2,1,0:T(8,128)(2,1)S(1)} %bitcast.102, bf16[2,1,2,128,128]{4,3,2,1,0:T(8,128)(2,1)S(1)} %collective-permute-done.refs_1_, ...), custom_call_target="tpu_custom_call" | custom-call | flops 1677721600 | bytes 8388608 | tf_op jit(solution)/shard_map/attend/pallas_call | solution.py:73
  26.6 2.6 %collective-permute-done.7 = bf16[4,256,512]{2,1,0:T(8,128)(2,1)S(1)} collective-permute-done((bf16[4,256,512]{2,1,0:T(8,128)(2,1)S(1)}, bf16[4,256,512]{2,1,0:T(8,128)(2,1)S(1)}, u32[]{:S(2)}, u32[]{:S(2)}) %collective-permute-start.7) | collective-permute-done | bytes 1048608 | tf_op jit(solution)/shard_map/ppermute | solution.py:19
  29.6 1.6 collective-permute-start.8
  31.7 1.5 collective-permute-start.10
  33.1 2.6 %collective-permute-start.12 = (s32[256,2]{0,1:T(2,128)S(1)}, s32[256,2]{0,1:T(2,128)S(1)}, u32[]{:S(2)}, u32[]{:S(2)}) collective-permute-start(s32[256,2]{0,1:T(2,128)S(1)} %copy-done.10), channel_id=1, source_target_pairs={{0,16},{8,24},{16,0},{24,8},{1,17},{9,25},{17,1},{25,9},{2,18},{10... | collective-permute-start | bytes 6152 | tf_op jit(solution)/shard_map/ppermute | solution.py:19
  36.3 1.3 collective-permute-done.12
  37.6 1.6 collective-permute-start.13
  39.3 4.7 %collective-permute-done.13.refs_4_ = s32[256,2]{1,0:T(8,128)S(1)} collective-permute-done((s32[256,2]{1,0:T(8,128)S(1)}, s32[256,2]{1,0:T(8,128)S(1)}, u32[]{:S(2)}, u32[]{:S(2)}) %collective-permute-start.13) | collective-permute-done | bytes 2080 | tf_op jit(solution)/shard_map/ppermute | solution.py:19
  45.7 2.6 %collective-permute-start.18 = (bf16[256,512]{1,0:T(8,128)(2,1)}, bf16[256,512]{1,0:T(8,128)(2,1)S(1)}, u32[]{:S(2)}, u32[]{:S(2)}) collective-permute-start(bf16[256,512]{1,0:T(8,128)(2,1)} %add_convert_fusion.14), channel_id=1, source_target_pairs={{0,16},{8,24},{16,0},{24,8},{1,17},{9,25},{17,1},{25,9},{2,18},{10... | collective-permute-start | bytes 786440 | tf_op jit(solution)/shard_map/ppermute | solution.py:19
  48.7 1.2 collective-permute-start.16
  50.8 1.4 collective-permute-start.14
  52.2 6.6 %collective-permute-done.18 = bf16[256,512]{1,0:T(8,128)(2,1)S(1)} collective-permute-done((bf16[256,512]{1,0:T(8,128)(2,1)}, bf16[256,512]{1,0:T(8,128)(2,1)S(1)}, u32[]{:S(2)}, u32[]{:S(2)}) %collective-permute-start.18) | collective-permute-done | bytes 262176 | tf_op jit(solution)/shard_map/ppermute | solution.py:19
  59.8 2.3 %collective-permute-done.15 = bf16[256,512]{1,0:T(8,128)(2,1)S(1)} collective-permute-done((bf16[256,512]{1,0:T(8,128)(2,1)}, bf16[256,512]{1,0:T(8,128)(2,1)S(1)}, u32[]{:S(2)}, u32[]{:S(2)}) %collective-permute-start.15) | collective-permute-done | bytes 262176 | tf_op jit(solution)/shard_map/ppermute | solution.py:19
  62.1 1.1 pad_maximum_fusion.1.refs_0_
  63.5 1.6 collective-permute-start.21
  65.6 1.4 collective-permute-start.19
  67.5 21.6 %units.3 = (bf16[256,1792]{1,0:T(8,128)(2,1)}, f32[256,128]{1,0:T(8,128)}, bf16[4,256,512]{2,1,0:T(8,128)(2,1)}, bf16[4,256,512]{2,1,0:T(8,128)(2,1)S(1)}) custom-call(s32[2]{0:T(128)S(1)} %pad_add_fusion.1.scalars_ref, bf16[4,256,512]{2,1,0:T(8,128)(2,1)S(1)} %pad_maximum_fusion.1.refs_0_, bf16[4,256,512]{2,1,0:T(8,128)(2,1)S(1)} %collective-permute-done.23.refs_1_, ...), custom_call_target="tpu_custom_call" | custom-call | flops 7516192768 | bytes 44040192 | tf_op jit(solution)/shard_map/units/pallas_call | solution.py:223
  90.0 1.6 pad_maximum_fusion.refs_0_
  92.3 4.9 %collective-permute-done.24 = bf16[4,256,512]{2,1,0:T(8,128)(2,1)S(1)} collective-permute-done((bf16[4,256,512]{2,1,0:T(8,128)(2,1)}, bf16[4,256,512]{2,1,0:T(8,128)(2,1)S(1)}, u32[]{:S(2)}, u32[]{:S(2)}) %collective-permute-start.24) | collective-permute-done | bytes 1048608 | tf_op jit(solution)/shard_map/ppermute | solution.py:19
  98.1 1.6 collective-permute-start.28
  100.2 1.4 collective-permute-start.26
  101.6 32.8 %units.4 = (bf16[512,1792]{1,0:T(8,128)(2,1)}, f32[512,128]{1,0:T(8,128)S(1)}, bf16[4,512,512]{2,1,0:T(8,128)(2,1)}, bf16[4,1792,512]{2,1,0:T(8,128)(2,1)S(1)}) custom-call(s32[2]{0:T(128)S(1)} %pad_add_fusion.1.scalars_ref, bf16[4,512,512]{2,1,0:T(8,128)(2,1)} %pad_maximum_fusion.refs_0_, bf16[4,512,512]{2,1,0:T(8,128)(2,1)} %collective-permute-done.25.refs_1_, ...), custom_call_target="tpu_custom_call" | custom-call | flops 15032385536 | bytes 44040192 | tf_op jit(solution)/shard_map/units/pallas_call | solution.py:223
  134.6 1.4 copy-done.12
  136.7 4.0 %down.2 = bf16[4,512,512]{2,1,0:T(8,128)(2,1)S(1)} custom-call(bf16[512,1792]{1,0:T(8,128)(2,1)S(1)} %copy-done.2, f32[512,128]{1,0:T(8,128)S(1)} %get-tuple-element.146.weight_ref, bf16[4,1792,512]{2,1,0:T(8,128)(2,1)S(1)} %get-tuple-element.147.down_ref), custom_call_target="tpu_custom_call" | custom-call | flops 3758096384 | bytes 7340032 | tf_op jit(solution)/shard_map/down/pallas_call | solution.py:254
  142.8 1.5 collective-permute-start.33
  144.9 1.4 collective-permute-start.31
  146.3 18.9 %units.5 = (bf16[256,1792]{1,0:T(8,128)(2,1)S(1)}, f32[256,128]{1,0:T(8,128)S(1)}, bf16[4,256,512]{2,1,0:T(8,128)(2,1)S(1)}, bf16[4,1792,512]{2,1,0:T(8,128)(2,1)S(1)}) custom-call(s32[2]{0:T(128)S(1)} %pad_add_fusion.1.scalars_ref, bf16[4,256,512]{2,1,0:T(8,128)(2,1)} %copy-done.3, bf16[4,256,512]{2,1,0:T(8,128)(2,1)} %copy-done.4, ...), custom_call_target="tpu_custom_call" | custom-call | flops 7516192768 | bytes 44040192 | tf_op jit(solution)/shard_map/units/pallas_call | solution.py:223
  165.2 3.7 %collective-permute-done.32 = bf16[512,512]{1,0:T(8,128)(2,1)S(1)} collective-permute-done((bf16[512,512]{1,0:T(8,128)(2,1)S(1)}, bf16[512,512]{1,0:T(8,128)(2,1)S(1)}, u32[]{:S(2)}, u32[]{:S(2)}) %collective-permute-start.32) | collective-permute-done | bytes 524320 | tf_op jit(solution)/shard_map/ppermute | solution.py:19
  168.9 2.1 %down.3 = bf16[4,256,512]{2,1,0:T(8,128)(2,1)S(1)} custom-call(bf16[256,1792]{1,0:T(8,128)(2,1)S(1)} %get-tuple-element.165.active_ref, f32[256,128]{1,0:T(8,128)S(1)} %get-tuple-element.166.weight_ref, bf16[4,1792,512]{2,1,0:T(8,128)(2,1)S(1)} %get-tuple-element.167.down_ref), custom_call_target="tpu_custom_call" | custom-call | flops 1879048192 | bytes 7340032 | tf_op jit(solution)/shard_map/down/pallas_call | solution.py:254
  172.5 1.4 collective-permute-start.39
  173.9 1.4 collective-permute-start.38
  175.6 1.6 collective-permute-start.34
  177.3 1.1 collective-permute-start.35
  178.4 2.6 %collective-permute-done.37 = bf16[256,512]{1,0:T(8,128)(2,1)S(1)} collective-permute-done((bf16[256,512]{1,0:T(8,128)(2,1)S(1)}, bf16[256,512]{1,0:T(8,128)(2,1)S(1)}, u32[]{:S(2)}, u32[]{:S(2)}) %collective-permute-start.37) | collective-permute-done | bytes 262176 | tf_op jit(solution)/shard_map/ppermute | solution.py:19
  181.0 5.0 %collective-permute-done.39 = bf16[256,512]{1,0:T(8,128)(2,1)S(1)} collective-permute-done((bf16[256,512]{1,0:T(8,128)(2,1)S(1)}, bf16[256,512]{1,0:T(8,128)(2,1)S(1)}, u32[]{:S(2)}, u32[]{:S(2)}) %collective-permute-start.39) | collective-permute-done | bytes 262176 | tf_op jit(solution)/shard_map/ppermute | solution.py:19
  186.0 1.4 collective-permute-done.38
  188.3 7.6 %collective-permute-done.35 = bf16[256,512]{1,0:T(8,128)(2,1)S(1)} collective-permute-done((bf16[256,512]{1,0:T(8,128)(2,1)S(1)}, bf16[256,512]{1,0:T(8,128)(2,1)S(1)}, u32[]{:S(2)}, u32[]{:S(2)}) %collective-permute-start.35) | collective-permute-done | bytes 262176 | tf_op jit(solution)/shard_map/ppermute | solution.py:19
  195.9 5.4 %collective-permute-done.40 = bf16[256,512]{1,0:T(8,128)(2,1)S(1)} collective-permute-done((bf16[256,512]{1,0:T(8,128)(2,1)S(1)}, bf16[256,512]{1,0:T(8,128)(2,1)S(1)}, u32[]{:S(2)}, u32[]{:S(2)}) %collective-permute-start.40) | collective-permute-done | bytes 262176 | tf_op jit(solution)/shard_map/ppermute | solution.py:19
  201.3 1.9 add_convert_fusion.5
  (102 shorter events, 17.6 us)
Async XLA Ops:
  1.4 5.9 %copy-start.11 = (bf16[4096]{0:T(1024)(128)(2,1)S(1)}, bf16[4096]{0:T(1024)(128)(2,1)}, u32[]{:S(2)}) copy-start(bf16[4096]{0:T(1024)(128)(2,1)} %param.22) | copy-start | bytes 24580
  1.5 5.9 %copy-start.9 = (bf16[4096,4]{0,1:T(4,128)(2,1)S(1)}, bf16[4096,4]{0,1:T(4,128)(2,1)}, u32[]{:S(2)}) copy-start(bf16[4096,4]{0,1:T(4,128)(2,1)} %param.23) | copy-start | bytes 98308
  1.5 14.9 %copy-start.7 = (bf16[256,4,128]{2,1,0:T(4,128)(2,1)S(1)}, bf16[256,4,128]{2,1,0:T(4,128)(2,1)}, u32[]{:S(2)}) copy-start(bf16[256,4,128]{2,1,0:T(4,128)(2,1)} %param.14) | copy-start | bytes 786436
  1.5 6.3 %collective-permute-start.5 = (bf16[2,1,2,128,128]{4,3,2,1,0:T(8,128)(2,1)S(1)}, bf16[2,1,2,128,128]{4,3,2,1,0:T(8,128)(2,1)S(1)}, u32[]{:S(2)}, u32[]{:S(2)}) collective-permute-start(bf16[2,1,2,128,128]{4,3,2,1,0:T(8,128)(2,1)S(1)} %get-tuple-element.192), channel_id=1, source_target_pairs={{0,6},{1,7},{2,4},{3,5},{4,2},{5,3},{6,0},{7,1},{8,14},{9,15},{10,... | collective-permute-start | bytes 393224 | tf_op jit(solution)/shard_map/ppermute | solution.py:19
  4.0 9.3 %collective-permute-start.4 = (bf16[2,1,2,128,128]{4,3,2,1,0:T(8,128)(2,1)S(1)}, bf16[2,1,2,128,128]{4,3,2,1,0:T(8,128)(2,1)S(1)}, u32[]{:S(2)}, u32[]{:S(2)}) collective-permute-start(bf16[2,1,2,128,128]{4,3,2,1,0:T(8,128)(2,1)S(1)} %get-tuple-element.193), channel_id=1, source_target_pairs={{0,5},{1,4},{2,7},{3,6},{4,1},{5,0},{6,3},{7,2},{8,13},{9,12},{10,... | collective-permute-start | bytes 393224 | tf_op jit(solution)/shard_map/ppermute | solution.py:19
  4.1 16.3 %collective-permute-start.6 = (bf16[2,1,2,128,128]{4,3,2,1,0:T(8,128)(2,1)S(1)}, bf16[2,1,2,128,128]{4,3,2,1,0:T(8,128)(2,1)S(1)}, u32[]{:S(2)}, u32[]{:S(2)}) collective-permute-start(bf16[2,1,2,128,128]{4,3,2,1,0:T(8,128)(2,1)S(1)} %get-tuple-element.186), channel_id=1, source_target_pairs={{0,7},{1,6},{2,5},{3,4},{4,3},{5,2},{6,1},{7,0},{8,15},{9,14},{10,... | collective-permute-start | bytes 393224 | tf_op jit(solution)/shard_map/ppermute | solution.py:19
  5.9 14.5 %collective-permute-start = (bf16[2,1,2,128,128]{4,3,2,1,0:T(8,128)(2,1)S(1)}, bf16[2,1,2,128,128]{4,3,2,1,0:T(8,128)(2,1)S(1)}, u32[]{:S(2)}, u32[]{:S(2)}) collective-permute-start(bf16[2,1,2,128,128]{4,3,2,1,0:T(8,128)(2,1)S(1)} %get-tuple-element.188), channel_id=1, source_target_pairs={{0,1},{1,0},{2,3},{3,2},{4,5},{5,4},{6,7},{7,6},{8,9},{9,8},{10,11... | collective-permute-start | bytes 393224 | tf_op jit(solution)/shard_map/ppermute | solution.py:19
  5.9 14.5 %collective-permute-start.1 = (bf16[2,1,2,128,128]{4,3,2,1,0:T(8,128)(2,1)S(1)}, bf16[2,1,2,128,128]{4,3,2,1,0:T(8,128)(2,1)S(1)}, u32[]{:S(2)}, u32[]{:S(2)}) collective-permute-start(bf16[2,1,2,128,128]{4,3,2,1,0:T(8,128)(2,1)S(1)} %get-tuple-element.189), channel_id=1, source_target_pairs={{0,2},{1,3},{2,0},{3,1},{4,6},{5,7},{6,4},{7,5},{8,10},{9,11},{10,... | collective-permute-start | bytes 393224 | tf_op jit(solution)/shard_map/ppermute | solution.py:19
  7.8 12.5 %collective-permute-start.2 = (bf16[2,1,2,128,128]{4,3,2,1,0:T(8,128)(2,1)S(1)}, bf16[2,1,2,128,128]{4,3,2,1,0:T(8,128)(2,1)S(1)}, u32[]{:S(2)}, u32[]{:S(2)}) collective-permute-start(bf16[2,1,2,128,128]{4,3,2,1,0:T(8,128)(2,1)S(1)} %get-tuple-element.190), channel_id=1, source_target_pairs={{0,3},{1,2},{2,1},{3,0},{4,7},{5,6},{6,5},{7,4},{8,11},{9,10},{10,... | collective-permute-start | bytes 393224 | tf_op jit(solution)/shard_map/ppermute | solution.py:19
  13.3 7.1 %collective-permute-start.3 = (bf16[2,1,2,128,128]{4,3,2,1,0:T(8,128)(2,1)S(1)}, bf16[2,1,2,128,128]{4,3,2,1,0:T(8,128)(2,1)S(1)}, u32[]{:S(2)}, u32[]{:S(2)}) collective-permute-start(bf16[2,1,2,128,128]{4,3,2,1,0:T(8,128)(2,1)S(1)} %get-tuple-element.191), channel_id=1, source_target_pairs={{0,4},{1,5},{2,6},{3,7},{4,0},{5,1},{6,2},{7,3},{8,12},{9,13},{10,... | collective-permute-start | bytes 393224 | tf_op jit(solution)/shard_map/ppermute | solution.py:19
  26.5 6.6 %copy-start.10 = (s32[256,2]{0,1:T(2,128)S(1)}, s32[256,2]{0,1:T(2,128)}, u32[]{:S(2)}) copy-start(s32[256,2]{0,1:T(2,128)} %param.24) | copy-start | bytes 6148
  26.5 18.3 %copy-start.8 = (bf16[256,512]{1,0:T(8,128)(2,1)S(1)}, bf16[256,512]{1,0:T(8,128)(2,1)}, u32[]{:S(2)}) copy-start(bf16[256,512]{1,0:T(8,128)(2,1)} %param.20) | copy-start | bytes 786436
  26.5 2.7 %collective-permute-start.7 = (bf16[4,256,512]{2,1,0:T(8,128)(2,1)S(1)}, bf16[4,256,512]{2,1,0:T(8,128)(2,1)S(1)}, u32[]{:S(2)}, u32[]{:S(2)}) collective-permute-start(bf16[4,256,512]{2,1,0:T(8,128)(2,1)S(1)} %get-tuple-element.102), channel_id=1, source_target_pairs={{0,1},{1,0},{2,3},{3,2},{4,5},{5,4},{6,7},{7,6},{8,9},{9,8},{10,11... | collective-permute-start | bytes 3145736 | tf_op jit(solution)/shard_map/ppermute | solution.py:19
  29.6 14.4 %collective-permute-start.8 = (bf16[256,512]{1,0:T(8,128)(2,1)S(1)}, bf16[256,512]{1,0:T(8,128)(2,1)S(1)}, u32[]{:S(2)}, u32[]{:S(2)}) collective-permute-start(bf16[256,512]{1,0:T(8,128)(2,1)S(1)} %get-tuple-element.104), channel_id=1, source_target_pairs={{0,2},{1,3},{2,0},{3,1},{4,6},{5,7},{6,4},{7,5},{8,10},{9,11},{10,... | collective-permute-start | bytes 786440 | tf_op jit(solution)/shard_map/ppermute | solution.py:19
  31.1 13.7 %collective-permute-start.9 = (bf16[256,512]{1,0:T(8,128)(2,1)S(1)}, bf16[256,512]{1,0:T(8,128)(2,1)S(1)}, u32[]{:S(2)}, u32[]{:S(2)}) collective-permute-start(bf16[256,512]{1,0:T(8,128)(2,1)S(1)} %get-tuple-element.105), channel_id=1, source_target_pairs={{0,4},{1,5},{2,6},{3,7},{4,0},{5,1},{6,2},{7,3},{8,12},{9,13},{10,... | collective-permute-start | bytes 786440 | tf_op jit(solution)/shard_map/ppermute | solution.py:19
  31.7 13.2 %collective-permute-start.10 = (bf16[256,512]{1,0:T(8,128)(2,1)S(1)}, bf16[256,512]{1,0:T(8,128)(2,1)S(1)}, u32[]{:S(2)}, u32[]{:S(2)}) collective-permute-start(bf16[256,512]{1,0:T(8,128)(2,1)S(1)} %get-tuple-element.106), channel_id=1, source_target_pairs={{0,6},{1,7},{2,4},{3,5},{4,2},{5,3},{6,0},{7,1},{8,14},{9,15},{10,... | collective-permute-start | bytes 786440 | tf_op jit(solution)/shard_map/ppermute | solution.py:19
  33.1 4.5 %collective-permute-start.12 = (s32[256,2]{0,1:T(2,128)S(1)}, s32[256,2]{0,1:T(2,128)S(1)}, u32[]{:S(2)}, u32[]{:S(2)}) collective-permute-start(s32[256,2]{0,1:T(2,128)S(1)} %copy-done.10), channel_id=1, source_target_pairs={{0,16},{8,24},{16,0},{24,8},{1,17},{9,25},{17,1},{25,9},{2,18},{10... | collective-permute-start | bytes 6152 | tf_op jit(solution)/shard_map/ppermute | solution.py:19
  35.7 3.6 %collective-permute-start.11 = (s32[256,2]{0,1:T(2,128)S(1)}, s32[256,2]{0,1:T(2,128)S(1)}, u32[]{:S(2)}, u32[]{:S(2)}) collective-permute-start(s32[256,2]{0,1:T(2,128)S(1)} %copy-done.10), channel_id=1, source_target_pairs={{0,8},{8,0},{16,24},{24,16},{1,9},{9,1},{17,25},{25,17},{2,10},{10... | collective-permute-start | bytes 6152 | tf_op jit(solution)/shard_map/ppermute | solution.py:19
  37.6 6.4 %collective-permute-start.13 = (s32[256,2]{1,0:T(8,128)S(1)}, s32[256,2]{1,0:T(8,128)S(1)}, u32[]{:S(2)}, u32[]{:S(2)}) collective-permute-start(s32[256,2]{1,0:T(8,128)S(1)} %copy.57), channel_id=1, source_target_pairs={{0,24},{8,16},{16,8},{24,0},{1,25},{9,17},{17,9},{25,1},{2,26},{10... | collective-permute-start | bytes 6152 | tf_op jit(solution)/shard_map/ppermute | solution.py:19
  45.7 13.1 %collective-permute-start.18 = (bf16[256,512]{1,0:T(8,128)(2,1)}, bf16[256,512]{1,0:T(8,128)(2,1)S(1)}, u32[]{:S(2)}, u32[]{:S(2)}) collective-permute-start(bf16[256,512]{1,0:T(8,128)(2,1)} %add_convert_fusion.14), channel_id=1, source_target_pairs={{0,16},{8,24},{16,0},{24,8},{1,17},{9,25},{17,1},{25,9},{2,18},{10... | collective-permute-start | bytes 786440 | tf_op jit(solution)/shard_map/ppermute | solution.py:19
  48.3 11.5 %collective-permute-start.17 = (bf16[256,512]{1,0:T(8,128)(2,1)}, bf16[256,512]{1,0:T(8,128)(2,1)S(1)}, u32[]{:S(2)}, u32[]{:S(2)}) collective-permute-start(bf16[256,512]{1,0:T(8,128)(2,1)} %add_convert_fusion.14), channel_id=1, source_target_pairs={{0,8},{8,0},{16,24},{24,16},{1,9},{9,1},{17,25},{25,17},{2,10},{10... | collective-permute-start | bytes 786440 | tf_op jit(solution)/shard_map/ppermute | solution.py:19
  48.7 11.0 %collective-permute-start.16 = (bf16[256,512]{1,0:T(8,128)(2,1)}, bf16[256,512]{1,0:T(8,128)(2,1)S(1)}, u32[]{:S(2)}, u32[]{:S(2)}) collective-permute-start(bf16[256,512]{1,0:T(8,128)(2,1)} %add_convert_fusion.14), channel_id=1, source_target_pairs={{0,6},{1,7},{2,4},{3,5},{4,2},{5,3},{6,0},{7,1},{8,14},{9,15},{10,... | collective-permute-start | bytes 786440 | tf_op jit(solution)/shard_map/ppermute | solution.py:19
  49.9 12.2 %collective-permute-start.15 = (bf16[256,512]{1,0:T(8,128)(2,1)}, bf16[256,512]{1,0:T(8,128)(2,1)S(1)}, u32[]{:S(2)}, u32[]{:S(2)}) collective-permute-start(bf16[256,512]{1,0:T(8,128)(2,1)} %add_convert_fusion.14), channel_id=1, source_target_pairs={{0,4},{1,5},{2,6},{3,7},{4,0},{5,1},{6,2},{7,3},{8,12},{9,13},{10,... | collective-permute-start | bytes 786440 | tf_op jit(solution)/shard_map/ppermute | solution.py:19
  50.8 11.3 %collective-permute-start.14 = (bf16[256,512]{1,0:T(8,128)(2,1)}, bf16[256,512]{1,0:T(8,128)(2,1)S(1)}, u32[]{:S(2)}, u32[]{:S(2)}) collective-permute-start(bf16[256,512]{1,0:T(8,128)(2,1)} %add_convert_fusion.14), channel_id=1, source_target_pairs={{0,2},{1,3},{2,0},{3,1},{4,6},{5,7},{6,4},{7,5},{8,10},{9,11},{10,... | collective-permute-start | bytes 786440 | tf_op jit(solution)/shard_map/ppermute | solution.py:19
  63.2 4.3 %collective-permute-start.23 = (bf16[4,256,512]{2,1,0:T(8,128)(2,1)S(1)}, bf16[4,256,512]{2,1,0:T(8,128)(2,1)S(1)}, u32[]{:S(2)}, u32[]{:S(2)}) collective-permute-start(bf16[4,256,512]{2,1,0:T(8,128)(2,1)S(1)} %pad_maximum_fusion.1.refs_0_), channel_id=1, source_target_pairs={{0,1},{1,0},{2,3},{3,2},{4,5},{5,4},{6,7},{7,6},{8,9},{9,8},{10,11... | collective-permute-start | bytes 3145736 | tf_op jit(solution)/shard_map/ppermute | solution.py:19
  63.5 25.6 %collective-permute-start.21 = (bf16[512,512]{1,0:T(8,128)(2,1)S(1)}, bf16[512,512]{1,0:T(8,128)(2,1)S(1)}, u32[]{:S(2)}, u32[]{:S(2)}) collective-permute-start(bf16[512,512]{1,0:T(8,128)(2,1)S(1)} %constant_dynamic-update-slice_fusion), channel_id=1, source_target_pairs={{0,6},{1,7},{2,4},{3,5},{4,2},{5,3},{6,0},{7,1},{8,14},{9,15},{10,... | collective-permute-start | bytes 1572872 | tf_op jit(solution)/shard_map/ppermute | solution.py:19
  65.0 25.0 %collective-permute-start.20 = (bf16[512,512]{1,0:T(8,128)(2,1)S(1)}, bf16[512,512]{1,0:T(8,128)(2,1)S(1)}, u32[]{:S(2)}, u32[]{:S(2)}) collective-permute-start(bf16[512,512]{1,0:T(8,128)(2,1)S(1)} %constant_dynamic-update-slice_fusion), channel_id=1, source_target_pairs={{0,4},{1,5},{2,6},{3,7},{4,0},{5,1},{6,2},{7,3},{8,12},{9,13},{10,... | collective-permute-start | bytes 1572872 | tf_op jit(solution)/shard_map/ppermute | solution.py:19
  65.6 24.4 %collective-permute-start.19 = (bf16[512,512]{1,0:T(8,128)(2,1)S(1)}, bf16[512,512]{1,0:T(8,128)(2,1)S(1)}, u32[]{:S(2)}, u32[]{:S(2)}) collective-permute-start(bf16[512,512]{1,0:T(8,128)(2,1)S(1)} %constant_dynamic-update-slice_fusion), channel_id=1, source_target_pairs={{0,2},{1,3},{2,0},{3,1},{4,6},{5,7},{6,4},{7,5},{8,10},{9,11},{10,... | collective-permute-start | bytes 1572872 | tf_op jit(solution)/shard_map/ppermute | solution.py:19
  67.0 22.1 %collective-permute-start.22 = (bf16[256,512]{1,0:T(8,128)(2,1)}, bf16[256,512]{1,0:T(8,128)(2,1)S(1)}, u32[]{:S(2)}, u32[]{:S(2)}) collective-permute-start(bf16[256,512]{1,0:T(8,128)(2,1)} %add_convert_fusion.14), channel_id=1, source_target_pairs={{0,24},{8,16},{16,8},{24,0},{1,25},{9,17},{17,9},{25,1},{2,26},{10... | collective-permute-start | bytes 786440 | tf_op jit(solution)/shard_map/ppermute | solution.py:19
  91.6 6.0 %collective-permute-start.25 = (bf16[4,512,512]{2,1,0:T(8,128)(2,1)}, bf16[4,512,512]{2,1,0:T(8,128)(2,1)}, u32[]{:S(2)}, u32[]{:S(2)}) collective-permute-start(bf16[4,512,512]{2,1,0:T(8,128)(2,1)} %pad_maximum_fusion.refs_0_), channel_id=1, source_target_pairs={{0,1},{1,0},{2,3},{3,2},{4,5},{5,4},{6,7},{7,6},{8,9},{9,8},{10,11... | collective-permute-start | bytes 6291464 | tf_op jit(solution)/shard_map/ppermute | solution.py:19
  91.6 5.5 %collective-permute-start.24 = (bf16[4,256,512]{2,1,0:T(8,128)(2,1)}, bf16[4,256,512]{2,1,0:T(8,128)(2,1)S(1)}, u32[]{:S(2)}, u32[]{:S(2)}) collective-permute-start(bf16[4,256,512]{2,1,0:T(8,128)(2,1)} %get-tuple-element.125), channel_id=1, source_target_pairs={{0,1},{1,0},{2,3},{3,2},{4,5},{5,4},{6,7},{7,6},{8,9},{9,8},{10,11... | collective-permute-start | bytes 3145736 | tf_op jit(solution)/shard_map/ppermute | solution.py:19
  92.3 5.6 %copy-start.6 = (bf16[256,512]{1,0:T(8,128)(2,1)S(1)}, bf16[256,512]{1,0:T(8,128)(2,1)}, u32[]{:S(2)}) copy-start(bf16[256,512]{1,0:T(8,128)(2,1)} %copy-done.5) | copy-start | bytes 786436
  98.1 36.4 %collective-permute-start.28 = (bf16[512,512]{1,0:T(8,128)(2,1)S(1)}, bf16[512,512]{1,0:T(8,128)(2,1)S(1)}, u32[]{:S(2)}, u32[]{:S(2)}) collective-permute-start(bf16[512,512]{1,0:T(8,128)(2,1)S(1)} %get-tuple-element.202), channel_id=1, source_target_pairs={{0,6},{1,7},{2,4},{3,5},{4,2},{5,3},{6,0},{7,1},{8,14},{9,15},{10,... | collective-permute-start | bytes 1572872 | tf_op jit(solution)/shard_map/ppermute | solution.py:19
  99.6 34.9 %collective-permute-start.27 = (bf16[512,512]{1,0:T(8,128)(2,1)S(1)}, bf16[512,512]{1,0:T(8,128)(2,1)S(1)}, u32[]{:S(2)}, u32[]{:S(2)}) collective-permute-start(bf16[512,512]{1,0:T(8,128)(2,1)S(1)} %get-tuple-element.203), channel_id=1, source_target_pairs={{0,4},{1,5},{2,6},{3,7},{4,0},{5,1},{6,2},{7,3},{8,12},{9,13},{10,... | collective-permute-start | bytes 1572872 | tf_op jit(solution)/shard_map/ppermute | solution.py:19
  100.2 34.3 %collective-permute-start.26 = (bf16[512,512]{1,0:T(8,128)(2,1)S(1)}, bf16[512,512]{1,0:T(8,128)(2,1)S(1)}, u32[]{:S(2)}, u32[]{:S(2)}) collective-permute-start(bf16[512,512]{1,0:T(8,128)(2,1)S(1)} %get-tuple-element.204), channel_id=1, source_target_pairs={{0,2},{1,3},{2,0},{3,1},{4,6},{5,7},{6,4},{7,5},{8,10},{9,11},{10,... | collective-permute-start | bytes 1572872 | tf_op jit(solution)/shard_map/ppermute | solution.py:19
  136.0 5.7 %collective-permute-start.29 = (bf16[4,512,512]{2,1,0:T(8,128)(2,1)S(1)}, bf16[4,512,512]{2,1,0:T(8,128)(2,1)S(1)}, u32[]{:S(2)}, u32[]{:S(2)}) collective-permute-start(bf16[4,512,512]{2,1,0:T(8,128)(2,1)S(1)} %copy-done.12), channel_id=1, source_target_pairs={{0,1},{1,0},{2,3},{3,2},{4,5},{5,4},{6,7},{7,6},{8,9},{9,8},{10,11... | collective-permute-start | bytes 6291464 | tf_op jit(solution)/shard_map/ppermute | solution.py:19
  136.1 4.5 %copy-start.3 = (bf16[4,256,512]{2,1,0:T(8,128)(2,1)}, bf16[4,256,512]{2,1,0:T(8,128)(2,1)S(1)}, u32[]{:S(2)}) copy-start(bf16[4,256,512]{2,1,0:T(8,128)(2,1)S(1)} %pad_maximum_fusion.2.refs_0_) | copy-start | bytes 3145732
  136.1 5.5 %collective-permute-start.30 = (bf16[4,256,512]{2,1,0:T(8,128)(2,1)S(1)}, bf16[4,256,512]{2,1,0:T(8,128)(2,1)S(1)}, u32[]{:S(2)}, u32[]{:S(2)}) collective-permute-start(bf16[4,256,512]{2,1,0:T(8,128)(2,1)S(1)} %pad_maximum_fusion.2.refs_0_), channel_id=1, source_target_pairs={{0,1},{1,0},{2,3},{3,2},{4,5},{5,4},{6,7},{7,6},{8,9},{9,8},{10,11... | collective-permute-start | bytes 3145736 | tf_op jit(solution)/shard_map/ppermute | solution.py:19
  142.8 22.4 %collective-permute-start.33 = (bf16[512,512]{1,0:T(8,128)(2,1)S(1)}, bf16[512,512]{1,0:T(8,128)(2,1)S(1)}, u32[]{:S(2)}, u32[]{:S(2)}) collective-permute-start(bf16[512,512]{1,0:T(8,128)(2,1)S(1)} %get-tuple-element.171), channel_id=1, source_target_pairs={{0,6},{1,7},{2,4},{3,5},{4,2},{5,3},{6,0},{7,1},{8,14},{9,15},{10,... | collective-permute-start | bytes 1572872 | tf_op jit(solution)/shard_map/ppermute | solution.py:19
  144.3 24.6 %collective-permute-start.32 = (bf16[512,512]{1,0:T(8,128)(2,1)S(1)}, bf16[512,512]{1,0:T(8,128)(2,1)S(1)}, u32[]{:S(2)}, u32[]{:S(2)}) collective-permute-start(bf16[512,512]{1,0:T(8,128)(2,1)S(1)} %get-tuple-element.172), channel_id=1, source_target_pairs={{0,4},{1,5},{2,6},{3,7},{4,0},{5,1},{6,2},{7,3},{8,12},{9,13},{10,... | collective-permute-start | bytes 1572872 | tf_op jit(solution)/shard_map/ppermute | solution.py:19
  144.9 24.0 %collective-permute-start.31 = (bf16[512,512]{1,0:T(8,128)(2,1)S(1)}, bf16[512,512]{1,0:T(8,128)(2,1)S(1)}, u32[]{:S(2)}, u32[]{:S(2)}) collective-permute-start(bf16[512,512]{1,0:T(8,128)(2,1)S(1)} %get-tuple-element.173), channel_id=1, source_target_pairs={{0,2},{1,3},{2,0},{3,1},{4,6},{5,7},{6,4},{7,5},{8,10},{9,11},{10,... | collective-permute-start | bytes 1572872 | tf_op jit(solution)/shard_map/ppermute | solution.py:19
  168.9 2.7 %collective-permute-start.36 = (bf16[4,256,512]{2,1,0:T(8,128)(2,1)S(1)}, bf16[4,256,512]{2,1,0:T(8,128)(2,1)S(1)}, u32[]{:S(2)}, u32[]{:S(2)}) collective-permute-start(bf16[4,256,512]{2,1,0:T(8,128)(2,1)S(1)} %get-tuple-element.168), channel_id=1, source_target_pairs={{0,1},{1,0},{2,3},{3,2},{4,5},{5,4},{6,7},{7,6},{8,9},{9,8},{10,11... | collective-permute-start | bytes 3145736 | tf_op jit(solution)/shard_map/ppermute | solution.py:19
  171.8 9.2 %collective-permute-start.37 = (bf16[256,512]{1,0:T(8,128)(2,1)S(1)}, bf16[256,512]{1,0:T(8,128)(2,1)S(1)}, u32[]{:S(2)}, u32[]{:S(2)}) collective-permute-start(bf16[256,512]{1,0:T(8,128)(2,1)S(1)} %get-tuple-element.175), channel_id=1, source_target_pairs={{0,2},{1,3},{2,0},{3,1},{4,6},{5,7},{6,4},{7,5},{8,10},{9,11},{10,... | collective-permute-start | bytes 786440 | tf_op jit(solution)/shard_map/ppermute | solution.py:19
  172.5 13.5 %collective-permute-start.39 = (bf16[256,512]{1,0:T(8,128)(2,1)S(1)}, bf16[256,512]{1,0:T(8,128)(2,1)S(1)}, u32[]{:S(2)}, u32[]{:S(2)}) collective-permute-start(bf16[256,512]{1,0:T(8,128)(2,1)S(1)} %get-tuple-element.176), channel_id=1, source_target_pairs={{0,6},{1,7},{2,4},{3,5},{4,2},{5,3},{6,0},{7,1},{8,14},{9,15},{10,... | collective-permute-start | bytes 786440 | tf_op jit(solution)/shard_map/ppermute | solution.py:19
  173.9 13.4 %collective-permute-start.38 = (bf16[256,512]{1,0:T(8,128)(2,1)S(1)}, bf16[256,512]{1,0:T(8,128)(2,1)S(1)}, u32[]{:S(2)}, u32[]{:S(2)}) collective-permute-start(bf16[256,512]{1,0:T(8,128)(2,1)S(1)} %get-tuple-element.177), channel_id=1, source_target_pairs={{0,4},{1,5},{2,6},{3,7},{4,0},{5,1},{6,2},{7,3},{8,12},{9,13},{10,... | collective-permute-start | bytes 786440 | tf_op jit(solution)/shard_map/ppermute | solution.py:19
  175.6 12.6 %collective-permute-start.34 = (bf16[256,512]{1,0:T(8,128)(2,1)S(1)}, bf16[256,512]{1,0:T(8,128)(2,1)S(1)}, u32[]{:S(2)}, u32[]{:S(2)}) collective-permute-start(bf16[256,512]{1,0:T(8,128)(2,1)S(1)} %get-tuple-element.194), channel_id=1, source_target_pairs={{0,8},{8,0},{16,24},{24,16},{1,9},{9,1},{17,25},{25,17},{2,10},{10... | collective-permute-start | bytes 786440 | tf_op jit(solution)/shard_map/ppermute | solution.py:19
  177.3 18.6 %collective-permute-start.35 = (bf16[256,512]{1,0:T(8,128)(2,1)S(1)}, bf16[256,512]{1,0:T(8,128)(2,1)S(1)}, u32[]{:S(2)}, u32[]{:S(2)}) collective-permute-start(bf16[256,512]{1,0:T(8,128)(2,1)S(1)} %get-tuple-element.195), channel_id=1, source_target_pairs={{0,16},{8,24},{16,0},{24,8},{1,17},{9,25},{17,1},{25,9},{2,18},{10... | collective-permute-start | bytes 786440 | tf_op jit(solution)/shard_map/ppermute | solution.py:19
  187.5 13.8 %collective-permute-start.40 = (bf16[256,512]{1,0:T(8,128)(2,1)S(1)}, bf16[256,512]{1,0:T(8,128)(2,1)S(1)}, u32[]{:S(2)}, u32[]{:S(2)}) collective-permute-start(bf16[256,512]{1,0:T(8,128)(2,1)S(1)} %fusion.6), channel_id=1, source_target_pairs={{0,24},{8,16},{16,8},{24,0},{1,25},{9,17},{17,9},{25,1},{2,26},{10... | collective-permute-start | bytes 786440 | tf_op jit(solution)/shard_map/ppermute | solution.py:19
  (6 other events, 12.5 us)
